TPU v7x, 32 devices: a whole 2x2x4 slice. The times are simulated.
32 devices in a mesh: groups: 1, blk: 32 (over z, y, x, core).
Axes of the slice: x: 2, y: 2, z: 4, core: 2. Of those that a mesh axis runs over, the one named last changes fastest.
Arguments:
- queries: float32 [256, 24576], P('groups', 'blk'), may hold values from -8 to 8
- cache: float32 [2048, 576], P(('groups', 'blk')), may hold values from -8 to 8
- owner: int32 [2048], P(('groups', 'blk')), may hold values from 0 to 1, as said below
- prefix_len: int32 [2], P('groups'), may hold values from 1 to 1152, as said below
- key_up: float32 [128, 512, 128], P('blk'), may hold values from -0.25 to 0.25
- value_up: float32 [128, 512, 128], P('blk'), may hold values from -0.25 to 0.25
- out_weight: float32 [16384, 7168], P('blk'), may hold values from -0.5 to 0.5
Outputs:
- mixed: float32 [256, 7168], P(('groups', 'blk'))
Inputs may be any that keep to these rules, and one draw needn't show every extreme that they name: `owner`: every request owns between 768 and 1280 slots, spread over the slots in no fixed order; some request owns exactly the fewest. prefix_len[r] + 128 is at most the number of slots that request r owns.
All inputs are finite; a program needn't handle non-finite values.
Results may differ from a plain program's by a relative error of at most 0.0003.
Values sent between devices are 32-bit elements; how exact they have to be, the bound alone decides.
A program may use at most 64 MiB of HBM per device.

v0:
```python
import math

import jax
import jax.numpy as jnp
from jax import lax
from jax.sharding import PartitionSpec as P

LATENT = 512
NOPE = 128
SPAN = 128
REQS = 2
CHUNKS = 4


def swap(x, bit, count):
    return lax.ppermute(x, "blk", [(i, i ^ (1 << bit)) for i in range(count)])


def bit_orders(count):
    bits = list(range(1, count.bit_length() - 1))
    low, high = bits[:2], bits[2:][::-1]
    return low + high, low[::-1] + high


def gather(block, me, count):
    rows = block.shape[0]
    parts = []
    for part, order in zip(jnp.split(block, 2, axis=0), bit_orders(count)):
        held, bits = part[None], []
        for bit in order[::-1] + [0]:
            other = swap(held, bit, count)
            mine = (me >> bit) & 1
            place = sum(1 for b in bits if b > bit)
            shape = (1 << place, -1) + part.shape
            a, b = held.reshape(shape), other.reshape(shape)
            first = jnp.where(mine == 0, a, b)
            second = jnp.where(mine == 0, b, a)
            held = jnp.stack([first, second], axis=1).reshape((-1,) + part.shape)
            bits.append(bit)
        parts.append(held)
    whole = jnp.stack(parts, axis=1)
    return whole.reshape(count * rows, block.shape[1])


def halves(x):
    high = lax.reduce_precision(x, 8, 7)
    return high.astype(jnp.bfloat16), (x - high).astype(jnp.bfloat16)


def split_weight(weight):
    width = weight.shape[1] // CHUNKS
    return [jnp.concatenate(halves(weight[:, c * width:(c + 1) * width]), axis=0) for c in range(CHUNKS)]


def project_and_scatter(flat, weights, me, count):
    rows, depth = flat.shape
    own = rows // count
    pairs = flat.reshape(count // 2, 2, own, depth)
    core = me & 1
    half = rows // 2
    away = lax.dynamic_index_in_dim(pairs, 1 - core, 1, keepdims=False).reshape(half, depth)
    home = lax.dynamic_index_in_dim(pairs, core, 1, keepdims=False).reshape(half, depth)
    split = []
    for x in (away, home):
        high, low = halves(x)
        split += [jnp.concatenate([high, high], axis=1), low]
    split = tuple(split)

    def dot(twice, low, both):
        left = jnp.dot(twice, both, preferred_element_type=jnp.float32)
        return left + jnp.dot(low, both[:depth], preferred_element_type=jnp.float32)

    orders = bit_orders(count)
    outs = []
    for c, both in enumerate(weights):
        width = both.shape[1]
        sent = dot(*split[:2], both)
        kept = dot(*split[2:], both)
        split, kept = lax.optimization_barrier((split, kept))
        left = kept + swap(sent, 0, count)
        bits = list(range(1, count.bit_length() - 1))
        for bit in orders[c % 2]:
            place = sum(1 for b in bits if b > bit)
            view = left.reshape(1 << place, 2, -1, own, width)
            mine = (me >> bit) & 1
            go = lax.dynamic_index_in_dim(view, 1 - mine, 1, keepdims=False).reshape(-1, width)
            stay = lax.dynamic_index_in_dim(view, mine, 1, keepdims=False).reshape(-1, width)
            left = stay + swap(go, bit, count)
            bits.remove(bit)
        outs.append(left)
    return jnp.concatenate(outs, axis=1)


def on_device(count, queries, cache, owner, prefix_len, key_up, value_up, out_weight):
    hp = lax.Precision.HIGH
    f32 = jnp.float32
    me = lax.axis_index("blk")
    heads = key_up.shape[0]
    rows = queries.shape[0]
    width = queries.shape[1] // heads
    block = jnp.concatenate([cache, owner.astype(f32)[:, None]], axis=1)
    weights = split_weight(out_weight)
    slab = gather(block, me, count)
    slots = slab.shape[0]
    keys = slab[:, :cache.shape[1]]
    latent = slab[:, :LATENT]
    owners = slab[:, cache.shape[1]].astype(jnp.int32)

    q3 = queries.reshape(rows, heads, width) * (1.0 / math.sqrt(width))
    q_latent = jnp.einsum("rhn,hln->hrl", q3[:, :, :NOPE], key_up, precision=hp, preferred_element_type=f32)
    q_all = jnp.concatenate([q_latent, jnp.transpose(q3[:, :, NOPE:], (1, 0, 2))], axis=2)

    lanes = math.gcd(slots, 128)
    req_ids = jnp.arange(REQS, dtype=jnp.int32)
    mine = owners[None, :] == req_ids[:, None]
    ones = mine.astype(f32).reshape(REQS, slots // lanes, lanes)
    lane = jnp.arange(lanes)
    before = (lane[:, None] < lane[None, :]).astype(f32)
    inside = jnp.einsum("rbl,lm->rbm", ones, before, precision=hp, preferred_element_type=f32)
    row = jnp.arange(slots // lanes)
    sums = jnp.sum(ones, axis=2)
    ahead = jnp.sum(jnp.where(row[None, None, :] < row[None, :, None], sums[:, None, :], 0.0), axis=2)
    position = (inside + ahead[:, :, None]).reshape(REQS, slots).astype(jnp.int32)
    rel = jnp.where(mine, position - prefix_len[:, None], jnp.int32(2**30))
    offset = jnp.arange(SPAN, dtype=jnp.int32)
    visible = (rel[:, None, :] <= offset[None, :, None]).reshape(1, rows, slots)

    score = jnp.einsum("hrl,tl->hrt", q_all, keys, precision=hp, preferred_element_type=f32)
    masked = jnp.where(visible, score, -jnp.inf)
    top = jnp.max(masked, axis=2, keepdims=True)
    expo = jnp.exp(masked - top)
    total = jnp.sum(expo, axis=2, keepdims=True)
    acc = jnp.einsum("hrt,tl->hrl", expo, latent, precision=hp, preferred_element_type=f32)
    head_out = jnp.einsum("hrl,hlv->hrv", acc / total, value_up, precision=hp, preferred_element_type=f32)
    flat = jnp.transpose(head_out, (1, 0, 2)).reshape(rows, heads * value_up.shape[2])
    return project_and_scatter(flat, weights, me, count)


def solution(mesh):
    count = mesh.shape["blk"]
    placed = (
        P("groups", "blk"),
        P(("groups", "blk"), None),
        P(("groups", "blk")),
        P("groups"),
        P("blk", None, None),
        P("blk", None, None),
        P("blk", None),
    )
    return jax.shard_map(
        lambda *args: on_device(count, *args),
        mesh=mesh,
        in_specs=placed,
        out_specs=P(("groups", "blk"), None),
        check_vma=False,
    )
```

profile of v0, /device:TPU:0, one launch (start us, length us, event | category | flops | bytes accessed | tf_op | source)
XLA Modules:
  0.0 165.8 jit_solution(5700976819847152699)
XLA Ops:
  1.8 3.0 %collective-permute-start = (f32[1,32,577]{2,1,0:T(8,128)S(1)}, f32[1,32,577]{2,1,0:T(8,128)S(1)}, u32[]{:S(2)}, u32[]{:S(2)}) collective-permute-start(f32[1,32,577]{2,1,0:T(8,128)S(1)} %fusion.56), channel_id=1, source_target_pairs={{0,8},{1,9},{2,10},{3,11},{4,12},{5,13},{6,14},{7,15},{8,0},{9,1},... | collective-permute-start | bytes 221576 | tf_op jit(solution)/shard_map/ppermute | solution.py:16
  4.8 2.4 %collective-permute-done = f32[1,32,577]{2,1,0:T(8,128)S(1)} collective-permute-done((f32[1,32,577]{2,1,0:T(8,128)S(1)}, f32[1,32,577]{2,1,0:T(8,128)S(1)}, u32[]{:S(2)}, u32[]{:S(2)}) %collective-permute-start) | collective-permute-done | bytes 73888 | tf_op jit(solution)/shard_map/ppermute | solution.py:16
  7.3 1.1 fusion.41
  8.3 2.1 %collective-permute-start.5 = (f32[1,32,577]{2,1,0:T(8,128)S(1)}, f32[1,32,577]{2,1,0:T(8,128)S(1)}, u32[]{:S(2)}, u32[]{:S(2)}) collective-permute-start(f32[1,32,577]{2,1,0:T(8,128)S(1)} %bitcast.277), channel_id=1, source_target_pairs={{0,8},{1,9},{2,10},{3,11},{4,12},{5,13},{6,14},{7,15},{8,0},{9,1},... | collective-permute-start | bytes 221576 | tf_op jit(solution)/shard_map/ppermute | solution.py:16
  10.4 2.7 %collective-permute-start.1 = (f32[2,32,577]{2,1,0:T(8,128)S(1)}, f32[2,32,577]{2,1,0:T(8,128)S(1)}, u32[]{:S(2)}, u32[]{:S(2)}) collective-permute-start(f32[2,32,577]{2,1,0:T(8,128)S(1)} %maximum_bitcast_fusion), channel_id=1, source_target_pairs={{0,16},{1,17},{2,18},{3,19},{4,20},{5,21},{6,22},{7,23},{8,24},{9,... | collective-permute-start | bytes 443144 | tf_op jit(solution)/shard_map/ppermute | solution.py:16
  13.6 3.0 %collective-permute-start.6 = (f32[2,32,577]{2,1,0:T(8,128)S(1)}, f32[2,32,577]{2,1,0:T(8,128)S(1)}, u32[]{:S(2)}, u32[]{:S(2)}) collective-permute-start(f32[2,32,577]{2,1,0:T(8,128)S(1)} %maximum_bitcast_fusion.1), channel_id=1, source_target_pairs={{0,16},{1,17},{2,18},{3,19},{4,20},{5,21},{6,22},{7,23},{8,24},{9,... | collective-permute-start | bytes 443144 | tf_op jit(solution)/shard_map/ppermute | solution.py:16
  16.6 7.3 %collective-permute-done.1 = f32[2,32,577]{2,1,0:T(8,128)S(1)} collective-permute-done((f32[2,32,577]{2,1,0:T(8,128)S(1)}, f32[2,32,577]{2,1,0:T(8,128)S(1)}, u32[]{:S(2)}, u32[]{:S(2)}) %collective-permute-start.1) | collective-permute-done | bytes 147744 | tf_op jit(solution)/shard_map/ppermute | solution.py:16
  23.9 2.5 %collective-permute-done.6 = f32[2,32,577]{2,1,0:T(8,128)S(1)} collective-permute-done((f32[2,32,577]{2,1,0:T(8,128)S(1)}, f32[2,32,577]{2,1,0:T(8,128)S(1)}, u32[]{:S(2)}, u32[]{:S(2)}) %collective-permute-start.6) | collective-permute-done | bytes 147744 | tf_op jit(solution)/shard_map/ppermute | solution.py:16
  26.5 1.6 collective-permute-start.2
  28.1 1.6 collective-permute-start.7
  29.7 5.7 %collective-permute-done.2 = f32[4,32,577]{2,1,0:T(8,128)S(1)} collective-permute-done((f32[4,32,577]{2,1,0:T(8,128)S(1)}, f32[4,32,577]{2,1,0:T(8,128)S(1)}, u32[]{:S(2)}, u32[]{:S(2)}) %collective-permute-start.2) | collective-permute-done | bytes 295456 | tf_op jit(solution)/shard_map/ppermute | solution.py:16
  36.3 1.5 collective-permute-start.3
  38.7 1.5 collective-permute-start.8
  40.3 10.4 %reduce-precision_convert_fusion = (bf16[512,1792]{1,0:T(8,128)(2,1)S(1)}, bf16[512,1792]{1,0:T(8,128)(2,1)}, bf16[512,1792]{1,0:T(8,128)(2,1)}, bf16[512,1792]{...) fusion(f32[512,7168]{1,0:T(8,128)} %param.13), kind=kLoop, calls=%fused_computation.5 | loop fusion | flops 14680064 | bytes 29360128 | tf_op jit(solution)/shard_map/convert_element_type | solution.py:47
  50.7 2.3 %copy.58 = f32[256,768]{0,1:T(8,128)} copy(f32[256,768]{1,0:T(8,128)} %param.7) | data formatting | bytes 1572864 | tf_op args[0]
  53.0 1.4 select_bitcast_fusion.5
  54.5 1.2 copy.52
  55.7 1.2 bitcast_select_fusion.1
  57.0 1.2 copy.55
  59.7 1.0 slice.38
  60.6 1.0 copy.66
  61.7 2.1 %fusion.30 = f32[4,256,512]{2,1,0:T(8,128)S(1)} fusion(f32[4,512,128]{2,1,0:T(8,128)S(1)} %copy-done, f32[256,4,192]{0,2,1:T(8,128)} %bitcast.255), kind=kOutput, calls=%fused_computation.70 | convolution fusion | flops 402653184 | bytes 3670016 | tf_op jit(solution)/shard_map/rhn,hln->hrl/dot_general | solution.py:110
  63.8 1.9 %select_bitcast_fusion.3 = (f32[16,1,1,32,577]{4,3,0,2,1:T(8,128)S(1)}, f32[16,1,1,32,577]{4,3,0,2,1:T(8,128)S(1)}) fusion(f32[16,32,577]{2,1,0:T(8,128)} %collective-permute-done.4, pred[]{:T(512)S(6)} %eq.55, f32[8,2,1,32,577]{4,3,1,0,2:T(8,128)} %copy.52), kind=kLoop, calls=%fused_computation.55 | loop fusion | flops 590848 | bytes 4726785 | tf_op jit(solution)/shard_map/stack | solution.py:38
  66.1 1.9 %select_bitcast_fusion.1 = (f32[16,1,1,32,577]{4,3,0,2,1:T(8,128)S(1)}, f32[16,1,1,32,577]{4,3,0,2,1:T(8,128)S(1)}) fusion(f32[16,32,577]{2,1,0:T(8,128)} %collective-permute-done.9, pred[]{:T(512)S(6)} %eq.55, f32[4,2,2,32,577]{4,3,2,1,0:T(8,128)} %copy.55), kind=kLoop, calls=%fused_computation.53 | loop fusion | flops 590848 | bytes 4726785 | tf_op jit(solution)/shard_map/stack | solution.py:38
  70.7 11.2 %select_reduce_fusion = (f32[4,256]{1,0:T(4,128)S(1)}, f32[4,256,2048]{2,1,0:T(8,128)S(1)}) fusion(pred[256,2048]{1,0:T(8,128)(4,1)S(1)} %broadcast_compare_fusion, f32[2048,577]{1,0:T(8,128)S(1)} %bitcast.246, f32[4,256,64]{2,1,0:T(8,128)S(1)} %bitcast.274, f32[4,256,512]{2,1,0:T(8,128)S(1)} %fusion.30), kind=kOutput, calls=%fused_computation.1 | convolution fusion | flops 7252540416 | bytes 16003072 | tf_op jit(solution)/shard_map/hrl,tl->hrt/dot_general | solution.py:128
  81.9 2.0 %fusion = f32[4,256]{1,0:T(4,128)S(1)} fusion(f32[4,256,2048]{2,1,0:T(8,128)S(1)} %get-tuple-element.75, f32[4,256]{1,0:T(4,128)S(1)} %get-tuple-element.74, pred[256,2048]{1,0:T(8,128)(4,1)S(1)} %broadcast_compare_fusion), kind=kLoop, calls=%fused_computation.2 | loop fusion | flops 6290432 | bytes 8921088 | tf_op jit(solution)/shard_map/reduce_sum | solution.py:132
  83.9 7.2 %fusion.1 = f32[4,256,512]{2,1,0:T(8,128)S(1)} fusion(f32[4,256,2048]{2,1,0:T(8,128)S(1)} %get-tuple-element.75, f32[2048,577]{1,0:T(8,128)S(1)} %bitcast.247, f32[4,256]{1,0:T(4,128)S(1)} %get-tuple-element.74, pred[256,2048]{1,0:T(8,128)(4,1)S(1)} %broadcast_compare_fusion), kind=kOutput, calls=%fused_computation.3 | convolution fusion | flops 6446645248 | bytes 15208448 | tf_op jit(solution)/shard_map/hrt,tl->hrl/dot_general | solution.py:133
  91.1 1.1 fusion.23
  92.9 2.8 %fusion.19 = f32[128,1792]{1,0:T(8,128)S(1)} fusion(bf16[512,1792]{1,0:T(8,128)(2,1)} %get-tuple-element.38, bf16[512,1792]{1,0:T(8,128)(2,1)} %get-tuple-element.43, bf16[128,512]{1,0:T(8,128)(2,1)S(1)} %get-tuple-element.64), kind=kOutput, calls=%fused_computation.46 | convolution fusion | flops 477626368 | bytes 4718592 | tf_op jit(solution)/shard_map/dot_general | solution.py:70
  97.7 1.0 copy-done.3
  102.1 1.1 copy-done.2
  107.0 1.1 copy-done.6
  112.1 1.0 collective-permute-start.16
  113.2 1.1 collective-permute-start.21
  114.6 1.6 collective-permute-start.26
  116.2 8.6 %collective-permute-done.11 = f32[64,1792]{1,0:T(8,128)S(1)} collective-permute-done((f32[64,1792]{1,0:T(8,128)S(1)}, f32[64,1792]{1,0:T(8,128)S(1)}, u32[]{:S(2)}, u32[]{:S(2)}) %collective-permute-start.11) | collective-permute-done | bytes 458784 | tf_op jit(solution)/shard_map/ppermute | solution.py:16
  125.6 1.6 collective-permute-start.17
  127.2 7.4 %collective-permute-done.21 = f32[64,1792]{1,0:T(8,128)S(1)} collective-permute-done((f32[64,1792]{1,0:T(8,128)S(1)}, f32[64,1792]{1,0:T(8,128)S(1)}, u32[]{:S(2)}, u32[]{:S(2)}) %collective-permute-start.21) | collective-permute-done | bytes 458784 | tf_op jit(solution)/shard_map/ppermute | solution.py:16
  135.4 1.6 collective-permute-start.27
  137.0 3.2 %collective-permute-done.12 = f32[32,1792]{1,0:T(8,128)S(1)} collective-permute-done((f32[32,1792]{1,0:T(8,128)S(1)}, f32[32,1792]{1,0:T(8,128)S(1)}, u32[]{:S(2)}, u32[]{:S(2)}) %collective-permute-start.12) | collective-permute-done | bytes 229408 | tf_op jit(solution)/shard_map/ppermute | solution.py:16
  140.5 3.0 %collective-permute-start.18 = (f32[16,1792]{1,0:T(8,128)S(1)}, f32[16,1792]{1,0:T(8,128)S(1)}, u32[]{:S(2)}, u32[]{:S(2)}) collective-permute-start(f32[16,1792]{1,0:T(8,128)S(1)} %dynamic-slice_bitcast_fusion.8), channel_id=1, source_target_pairs={{0,16},{1,17},{2,18},{3,19},{4,20},{5,21},{6,22},{7,23},{8,24},{9,... | collective-permute-start | bytes 344072 | tf_op jit(solution)/shard_map/ppermute | solution.py:16
  144.4 3.0 %collective-permute-start.28 = (f32[16,1792]{1,0:T(8,128)S(1)}, f32[16,1792]{1,0:T(8,128)S(1)}, u32[]{:S(2)}, u32[]{:S(2)}) collective-permute-start(f32[16,1792]{1,0:T(8,128)S(1)} %dynamic-slice_bitcast_fusion.6), channel_id=1, source_target_pairs={{0,16},{1,17},{2,18},{3,19},{4,20},{5,21},{6,22},{7,23},{8,24},{9,... | collective-permute-start | bytes 344072 | tf_op jit(solution)/shard_map/ppermute | solution.py:16
  147.3 7.5 %collective-permute-done.13 = f32[16,1792]{1,0:T(8,128)S(1)} collective-permute-done((f32[16,1792]{1,0:T(8,128)S(1)}, f32[16,1792]{1,0:T(8,128)S(1)}, u32[]{:S(2)}, u32[]{:S(2)}) %collective-permute-start.13) | collective-permute-done | bytes 114720 | tf_op jit(solution)/shard_map/ppermute | solution.py:16
  154.9 2.3 %collective-permute-done.18 = f32[16,1792]{1,0:T(8,128)S(1)} collective-permute-done((f32[16,1792]{1,0:T(8,128)S(1)}, f32[16,1792]{1,0:T(8,128)S(1)}, u32[]{:S(2)}, u32[]{:S(2)}) %collective-permute-start.18) | collective-permute-done | bytes 114720 | tf_op jit(solution)/shard_map/ppermute | solution.py:16
  157.4 2.2 %collective-permute-done.23 = f32[16,1792]{1,0:T(8,128)S(1)} collective-permute-done((f32[16,1792]{1,0:T(8,128)S(1)}, f32[16,1792]{1,0:T(8,128)S(1)}, u32[]{:S(2)}, u32[]{:S(2)}) %collective-permute-start.23) | collective-permute-done | bytes 114720 | tf_op jit(solution)/shard_map/ppermute | solution.py:16
  159.7 1.1 collective-permute-done.28
  162.1 1.2 collective-permute-done.19
  163.3 1.1 collective-permute-done.24
  (142 shorter events, 28.7 us)
Async XLA Ops:
  0.0 61.7 %copy-start = (f32[4,512,128]{2,1,0:T(8,128)S(1)}, f32[4,512,128]{2,1,0:T(8,128)}, u32[]{:S(2)}) copy-start(f32[4,512,128]{2,1,0:T(8,128)} %param.11) | copy-start | bytes 3145732
  1.8 5.5 %collective-permute-start = (f32[1,32,577]{2,1,0:T(8,128)S(1)}, f32[1,32,577]{2,1,0:T(8,128)S(1)}, u32[]{:S(2)}, u32[]{:S(2)}) collective-permute-start(f32[1,32,577]{2,1,0:T(8,128)S(1)} %fusion.56), channel_id=1, source_target_pairs={{0,8},{1,9},{2,10},{3,11},{4,12},{5,13},{6,14},{7,15},{8,0},{9,1},... | collective-permute-start | bytes 221576 | tf_op jit(solution)/shard_map/ppermute | solution.py:16
  8.3 5.2 %collective-permute-start.5 = (f32[1,32,577]{2,1,0:T(8,128)S(1)}, f32[1,32,577]{2,1,0:T(8,128)S(1)}, u32[]{:S(2)}, u32[]{:S(2)}) collective-permute-start(f32[1,32,577]{2,1,0:T(8,128)S(1)} %bitcast.277), channel_id=1, source_target_pairs={{0,8},{1,9},{2,10},{3,11},{4,12},{5,13},{6,14},{7,15},{8,0},{9,1},... | collective-permute-start | bytes 221576 | tf_op jit(solution)/shard_map/ppermute | solution.py:16
  10.4 13.5 %collective-permute-start.1 = (f32[2,32,577]{2,1,0:T(8,128)S(1)}, f32[2,32,577]{2,1,0:T(8,128)S(1)}, u32[]{:S(2)}, u32[]{:S(2)}) collective-permute-start(f32[2,32,577]{2,1,0:T(8,128)S(1)} %maximum_bitcast_fusion), channel_id=1, source_target_pairs={{0,16},{1,17},{2,18},{3,19},{4,20},{5,21},{6,22},{7,23},{8,24},{9,... | collective-permute-start | bytes 443144 | tf_op jit(solution)/shard_map/ppermute | solution.py:16
  13.6 12.8 %collective-permute-start.6 = (f32[2,32,577]{2,1,0:T(8,128)S(1)}, f32[2,32,577]{2,1,0:T(8,128)S(1)}, u32[]{:S(2)}, u32[]{:S(2)}) collective-permute-start(f32[2,32,577]{2,1,0:T(8,128)S(1)} %maximum_bitcast_fusion.1), channel_id=1, source_target_pairs={{0,16},{1,17},{2,18},{3,19},{4,20},{5,21},{6,22},{7,23},{8,24},{9,... | collective-permute-start | bytes 443144 | tf_op jit(solution)/shard_map/ppermute | solution.py:16
  26.5 8.8 %collective-permute-start.2 = (f32[4,32,577]{2,1,0:T(8,128)S(1)}, f32[4,32,577]{2,1,0:T(8,128)S(1)}, u32[]{:S(2)}, u32[]{:S(2)}) collective-permute-start(f32[4,32,577]{2,1,0:T(8,128)S(1)} %bitcast.264), channel_id=1, source_target_pairs={{0,4},{1,5},{2,6},{3,7},{4,0},{5,1},{6,2},{7,3},{8,12},{9,13},{10,... | collective-permute-start | bytes 886280 | tf_op jit(solution)/shard_map/ppermute | solution.py:16
  28.1 9.7 %collective-permute-start.7 = (f32[4,32,577]{2,1,0:T(8,128)S(1)}, f32[4,32,577]{2,1,0:T(8,128)S(1)}, u32[]{:S(2)}, u32[]{:S(2)}) collective-permute-start(f32[4,32,577]{2,1,0:T(8,128)S(1)} %bitcast.265), channel_id=1, source_target_pairs={{0,2},{1,3},{2,0},{3,1},{4,6},{5,7},{6,4},{7,5},{8,10},{9,11},{10,... | collective-permute-start | bytes 886280 | tf_op jit(solution)/shard_map/ppermute | solution.py:16
  36.3 16.7 %collective-permute-start.3 = (f32[8,32,577]{2,1,0:T(8,128)}, f32[8,32,577]{2,1,0:T(8,128)}, u32[]{:S(2)}, u32[]{:S(2)}) collective-permute-start(f32[8,32,577]{2,1,0:T(8,128)} %bitcast.13), channel_id=1, source_target_pairs={{0,2},{1,3},{2,0},{3,1},{4,6},{5,7},{6,4},{7,5},{8,10},{9,11},{10,... | collective-permute-start | bytes 1772552 | tf_op jit(solution)/shard_map/ppermute | solution.py:16
  38.7 16.9 %collective-permute-start.8 = (f32[8,32,577]{2,1,0:T(8,128)}, f32[8,32,577]{2,1,0:T(8,128)}, u32[]{:S(2)}, u32[]{:S(2)}) collective-permute-start(f32[8,32,577]{2,1,0:T(8,128)} %bitcast.32), channel_id=1, source_target_pairs={{0,4},{1,5},{2,6},{3,7},{4,0},{5,1},{6,2},{7,3},{8,12},{9,13},{10,... | collective-permute-start | bytes 1772552 | tf_op jit(solution)/shard_map/ppermute | solution.py:16
  55.7 8.1 %collective-permute-start.4 = (f32[16,32,577]{2,1,0:T(8,128)}, f32[16,32,577]{2,1,0:T(8,128)}, u32[]{:S(2)}, u32[]{:S(2)}) collective-permute-start(f32[16,32,577]{2,1,0:T(8,128)} %bitcast.16), channel_id=1, source_target_pairs={{0,1},{1,0},{2,3},{3,2},{4,5},{5,4},{6,7},{7,6},{8,9},{9,8},{10,11... | collective-permute-start | bytes 3545096 | tf_op jit(solution)/shard_map/ppermute | solution.py:16
  56.9 1.8 %copy-start.5 = (f32[256,768]{0,1:T(8,128)S(1)}, f32[256,768]{0,1:T(8,128)}, u32[]{:S(2)}) copy-start(f32[256,768]{0,1:T(8,128)} %copy.58) | copy-start | bytes 2359300
  58.2 7.9 %collective-permute-start.9 = (f32[16,32,577]{2,1,0:T(8,128)}, f32[16,32,577]{2,1,0:T(8,128)}, u32[]{:S(2)}, u32[]{:S(2)}) collective-permute-start(f32[16,32,577]{2,1,0:T(8,128)} %bitcast.34), channel_id=1, source_target_pairs={{0,1},{1,0},{2,3},{3,2},{4,5},{5,4},{6,7},{7,6},{8,9},{9,8},{10,11... | collective-permute-start | bytes 3545096 | tf_op jit(solution)/shard_map/ppermute | solution.py:16
  68.8 1.4 copy-start.11
  68.8 1.9 %copy-start.10 = (f32[256,4,64]{2,0,1:T(8,128)S(1)}, f32[256,4,64]{2,0,1:T(8,128)}, u32[]{:S(2)}) copy-start(f32[256,4,64]{2,0,1:T(8,128)} %copy.66) | copy-start | bytes 786436
  83.9 7.2 %copy-start.12 = (f32[4,512,128]{2,1,0:T(8,128)S(1)}, f32[4,512,128]{2,1,0:T(8,128)}, u32[]{:S(2)}) copy-start(f32[4,512,128]{2,1,0:T(8,128)} %param.12) | copy-start | bytes 3145732
  92.9 2.9 %copy-start.4 = (bf16[512,1792]{1,0:T(8,128)(2,1)S(1)}, bf16[512,1792]{1,0:T(8,128)(2,1)}, u32[]{:S(2)}) copy-start(bf16[512,1792]{1,0:T(8,128)(2,1)} %get-tuple-element.43) | copy-start | bytes 5505028
  92.9 3.1 %copy-start.9 = (bf16[512,1792]{1,0:T(8,128)(2,1)S(1)}, bf16[512,1792]{1,0:T(8,128)(2,1)}, u32[]{:S(2)}) copy-start(bf16[512,1792]{1,0:T(8,128)(2,1)} %get-tuple-element.38) | copy-start | bytes 5505028
  97.2 1.5 copy-start.3
  97.2 2.0 %copy-start.8 = (bf16[512,1792]{1,0:T(8,128)(2,1)S(1)}, bf16[512,1792]{1,0:T(8,128)(2,1)}, u32[]{:S(2)}) copy-start(bf16[512,1792]{1,0:T(8,128)(2,1)} %get-tuple-element.39) | copy-start | bytes 5505028
  97.2 13.9 %collective-permute-start.10 = (f32[128,1792]{1,0:T(8,128)S(1)}, f32[128,1792]{1,0:T(8,128)S(1)}, u32[]{:S(2)}, u32[]{:S(2)}) collective-permute-start(f32[128,1792]{1,0:T(8,128)S(1)} %convolution_add_fusion.6), channel_id=1, source_target_pairs={{0,1},{1,0},{2,3},{3,2},{4,5},{5,4},{6,7},{7,6},{8,9},{9,8},{10,11... | collective-permute-start | bytes 2752520 | tf_op jit(solution)/shard_map/ppermute | solution.py:16
  100.6 11.3 %collective-permute-start.15 = (f32[128,1792]{1,0:T(8,128)S(1)}, f32[128,1792]{1,0:T(8,128)S(1)}, u32[]{:S(2)}, u32[]{:S(2)}) collective-permute-start(f32[128,1792]{1,0:T(8,128)S(1)} %convolution_add_fusion.4), channel_id=1, source_target_pairs={{0,1},{1,0},{2,3},{3,2},{4,5},{5,4},{6,7},{7,6},{8,9},{9,8},{10,11... | collective-permute-start | bytes 2752520 | tf_op jit(solution)/shard_map/ppermute | solution.py:16
  101.6 1.5 copy-start.2
  101.7 2.0 %copy-start.7 = (bf16[512,1792]{1,0:T(8,128)(2,1)S(1)}, bf16[512,1792]{1,0:T(8,128)(2,1)}, u32[]{:S(2)}) copy-start(bf16[512,1792]{1,0:T(8,128)(2,1)} %get-tuple-element.40) | copy-start | bytes 5505028
  105.1 8.0 %collective-permute-start.20 = (f32[128,1792]{1,0:T(8,128)S(1)}, f32[128,1792]{1,0:T(8,128)S(1)}, u32[]{:S(2)}, u32[]{:S(2)}) collective-permute-start(f32[128,1792]{1,0:T(8,128)S(1)} %convolution_add_fusion.2), channel_id=1, source_target_pairs={{0,1},{1,0},{2,3},{3,2},{4,5},{5,4},{6,7},{7,6},{8,9},{9,8},{10,11... | collective-permute-start | bytes 2752520 | tf_op jit(solution)/shard_map/ppermute | solution.py:16
  106.5 1.5 copy-start.6
  109.4 4.9 %collective-permute-start.25 = (f32[128,1792]{1,0:T(8,128)S(1)}, f32[128,1792]{1,0:T(8,128)S(1)}, u32[]{:S(2)}, u32[]{:S(2)}) collective-permute-start(f32[128,1792]{1,0:T(8,128)S(1)} %convolution_add_fusion), channel_id=1, source_target_pairs={{0,1},{1,0},{2,3},{3,2},{4,5},{5,4},{6,7},{7,6},{8,9},{9,8},{10,11... | collective-permute-start | bytes 2752520 | tf_op jit(solution)/shard_map/ppermute | solution.py:16
  111.3 13.4 %collective-permute-start.11 = (f32[64,1792]{1,0:T(8,128)S(1)}, f32[64,1792]{1,0:T(8,128)S(1)}, u32[]{:S(2)}, u32[]{:S(2)}) collective-permute-start(f32[64,1792]{1,0:T(8,128)S(1)} %dynamic-slice_bitcast_fusion.1), channel_id=1, source_target_pairs={{0,2},{1,3},{2,0},{3,1},{4,6},{5,7},{6,4},{7,5},{8,10},{9,11},{10,... | collective-permute-start | bytes 1376264 | tf_op jit(solution)/shard_map/ppermute | solution.py:16
  112.1 13.5 %collective-permute-start.16 = (f32[64,1792]{1,0:T(8,128)S(1)}, f32[64,1792]{1,0:T(8,128)S(1)}, u32[]{:S(2)}, u32[]{:S(2)}) collective-permute-start(f32[64,1792]{1,0:T(8,128)S(1)} %bitcast.275), channel_id=1, source_target_pairs={{0,4},{1,5},{2,6},{3,7},{4,0},{5,1},{6,2},{7,3},{8,12},{9,13},{10,... | collective-permute-start | bytes 1376264 | tf_op jit(solution)/shard_map/ppermute | solution.py:16
  113.2 21.3 %collective-permute-start.21 = (f32[64,1792]{1,0:T(8,128)S(1)}, f32[64,1792]{1,0:T(8,128)S(1)}, u32[]{:S(2)}, u32[]{:S(2)}) collective-permute-start(f32[64,1792]{1,0:T(8,128)S(1)} %dynamic-slice_bitcast_fusion), channel_id=1, source_target_pairs={{0,2},{1,3},{2,0},{3,1},{4,6},{5,7},{6,4},{7,5},{8,10},{9,11},{10,... | collective-permute-start | bytes 1376264 | tf_op jit(solution)/shard_map/ppermute | solution.py:16
  114.6 20.8 %collective-permute-start.26 = (f32[64,1792]{1,0:T(8,128)S(1)}, f32[64,1792]{1,0:T(8,128)S(1)}, u32[]{:S(2)}, u32[]{:S(2)}) collective-permute-start(f32[64,1792]{1,0:T(8,128)S(1)} %bitcast.276), channel_id=1, source_target_pairs={{0,4},{1,5},{2,6},{3,7},{4,0},{5,1},{6,2},{7,3},{8,12},{9,13},{10,... | collective-permute-start | bytes 1376264 | tf_op jit(solution)/shard_map/ppermute | solution.py:16
  124.8 15.4 %collective-permute-start.12 = (f32[32,1792]{1,0:T(8,128)S(1)}, f32[32,1792]{1,0:T(8,128)S(1)}, u32[]{:S(2)}, u32[]{:S(2)}) collective-permute-start(f32[32,1792]{1,0:T(8,128)S(1)} %dynamic-slice_bitcast_fusion.5), channel_id=1, source_target_pairs={{0,4},{1,5},{2,6},{3,7},{4,0},{5,1},{6,2},{7,3},{8,12},{9,13},{10,... | collective-permute-start | bytes 688136 | tf_op jit(solution)/shard_map/ppermute | solution.py:16
  125.6 14.8 %collective-permute-start.17 = (f32[32,1792]{1,0:T(8,128)S(1)}, f32[32,1792]{1,0:T(8,128)S(1)}, u32[]{:S(2)}, u32[]{:S(2)}) collective-permute-start(f32[32,1792]{1,0:T(8,128)S(1)} %dynamic-slice_bitcast_fusion.4), channel_id=1, source_target_pairs={{0,2},{1,3},{2,0},{3,1},{4,6},{5,7},{6,4},{7,5},{8,10},{9,11},{10,... | collective-permute-start | bytes 688136 | tf_op jit(solution)/shard_map/ppermute | solution.py:16
  134.7 9.5 %collective-permute-start.22 = (f32[32,1792]{1,0:T(8,128)S(1)}, f32[32,1792]{1,0:T(8,128)S(1)}, u32[]{:S(2)}, u32[]{:S(2)}) collective-permute-start(f32[32,1792]{1,0:T(8,128)S(1)} %dynamic-slice_bitcast_fusion.3), channel_id=1, source_target_pairs={{0,4},{1,5},{2,6},{3,7},{4,0},{5,1},{6,2},{7,3},{8,12},{9,13},{10,... | collective-permute-start | bytes 688136 | tf_op jit(solution)/shard_map/ppermute | solution.py:16
  135.4 8.9 %collective-permute-start.27 = (f32[32,1792]{1,0:T(8,128)S(1)}, f32[32,1792]{1,0:T(8,128)S(1)}, u32[]{:S(2)}, u32[]{:S(2)}) collective-permute-start(f32[32,1792]{1,0:T(8,128)S(1)} %dynamic-slice_bitcast_fusion.2), channel_id=1, source_target_pairs={{0,2},{1,3},{2,0},{3,1},{4,6},{5,7},{6,4},{7,5},{8,10},{9,11},{10,... | collective-permute-start | bytes 688136 | tf_op jit(solution)/shard_map/ppermute | solution.py:16
  140.3 14.5 %collective-permute-start.13 = (f32[16,1792]{1,0:T(8,128)S(1)}, f32[16,1792]{1,0:T(8,128)S(1)}, u32[]{:S(2)}, u32[]{:S(2)}) collective-permute-start(f32[16,1792]{1,0:T(8,128)S(1)} %dynamic-slice_bitcast_fusion.9), channel_id=1, source_target_pairs={{0,16},{1,17},{2,18},{3,19},{4,20},{5,21},{6,22},{7,23},{8,24},{9,... | collective-permute-start | bytes 344072 | tf_op jit(solution)/shard_map/ppermute | solution.py:16
  140.4 25.4 %copy-start.1 = (f32[4,512,128]{2,1,0:T(8,128)S(1)}, f32[4,512,128]{2,1,0:T(8,128)}, u32[]{:S(2)}) copy-start(f32[4,512,128]{2,1,0:T(8,128)} %param.11) | copy-start | bytes 3145732
  140.5 16.8 %collective-permute-start.18 = (f32[16,1792]{1,0:T(8,128)S(1)}, f32[16,1792]{1,0:T(8,128)S(1)}, u32[]{:S(2)}, u32[]{:S(2)}) collective-permute-start(f32[16,1792]{1,0:T(8,128)S(1)} %dynamic-slice_bitcast_fusion.8), channel_id=1, source_target_pairs={{0,16},{1,17},{2,18},{3,19},{4,20},{5,21},{6,22},{7,23},{8,24},{9,... | collective-permute-start | bytes 344072 | tf_op jit(solution)/shard_map/ppermute | solution.py:16
  144.2 15.4 %collective-permute-start.23 = (f32[16,1792]{1,0:T(8,128)S(1)}, f32[16,1792]{1,0:T(8,128)S(1)}, u32[]{:S(2)}, u32[]{:S(2)}) collective-permute-start(f32[16,1792]{1,0:T(8,128)S(1)} %dynamic-slice_bitcast_fusion.7), channel_id=1, source_target_pairs={{0,16},{1,17},{2,18},{3,19},{4,20},{5,21},{6,22},{7,23},{8,24},{9,... | collective-permute-start | bytes 344072 | tf_op jit(solution)/shard_map/ppermute | solution.py:16
  144.4 16.5 %collective-permute-start.28 = (f32[16,1792]{1,0:T(8,128)S(1)}, f32[16,1792]{1,0:T(8,128)S(1)}, u32[]{:S(2)}, u32[]{:S(2)}) collective-permute-start(f32[16,1792]{1,0:T(8,128)S(1)} %dynamic-slice_bitcast_fusion.6), channel_id=1, source_target_pairs={{0,16},{1,17},{2,18},{3,19},{4,20},{5,21},{6,22},{7,23},{8,24},{9,... | collective-permute-start | bytes 344072 | tf_op jit(solution)/shard_map/ppermute | solution.py:16
  154.8 7.2 %collective-permute-start.14 = (f32[8,1792]{1,0:T(8,128)S(1)}, f32[8,1792]{1,0:T(8,128)S(1)}, u32[]{:S(2)}, u32[]{:S(2)}) collective-permute-start(f32[8,1792]{1,0:T(8,128)S(1)} %dynamic-slice_bitcast_fusion.13), channel_id=1, source_target_pairs={{0,8},{1,9},{2,10},{3,11},{4,12},{5,13},{6,14},{7,15},{8,0},{9,1},... | collective-permute-start | bytes 172040 | tf_op jit(solution)/shard_map/ppermute | solution.py:16
  157.3 6.0 %collective-permute-start.19 = (f32[8,1792]{1,0:T(8,128)S(1)}, f32[8,1792]{1,0:T(8,128)S(1)}, u32[]{:S(2)}, u32[]{:S(2)}) collective-permute-start(f32[8,1792]{1,0:T(8,128)S(1)} %dynamic-slice_bitcast_fusion.12), channel_id=1, source_target_pairs={{0,8},{1,9},{2,10},{3,11},{4,12},{5,13},{6,14},{7,15},{8,0},{9,1},... | collective-permute-start | bytes 172040 | tf_op jit(solution)/shard_map/ppermute | solution.py:16
  159.6 4.8 %collective-permute-start.24 = (f32[8,1792]{1,0:T(8,128)S(1)}, f32[8,1792]{1,0:T(8,128)S(1)}, u32[]{:S(2)}, u32[]{:S(2)}) collective-permute-start(f32[8,1792]{1,0:T(8,128)S(1)} %dynamic-slice_bitcast_fusion.11), channel_id=1, source_target_pairs={{0,8},{1,9},{2,10},{3,11},{4,12},{5,13},{6,14},{7,15},{8,0},{9,1},... | collective-permute-start | bytes 172040 | tf_op jit(solution)/shard_map/ppermute | solution.py:16
  160.9 4.2 %collective-permute-start.29 = (f32[8,1792]{1,0:T(8,128)S(1)}, f32[8,1792]{1,0:T(8,128)S(1)}, u32[]{:S(2)}, u32[]{:S(2)}) collective-permute-start(f32[8,1792]{1,0:T(8,128)S(1)} %dynamic-slice_bitcast_fusion.10), channel_id=1, source_target_pairs={{0,8},{1,9},{2,10},{3,11},{4,12},{5,13},{6,14},{7,15},{8,0},{9,1},... | collective-permute-start | bytes 172040 | tf_op jit(solution)/shard_map/ppermute | solution.py:16
where the time goes:
time: 166 us
  waiting for transfers between devices  55 us (33%)
  starting transfers between devices  34.3 us (21%)
  matrix products  34.2 us (21%)
  other arithmetic  28.5 us (17%)
  local copies, waits for them, and re-layouts  13.1 us (8%)
    ppermute x30, waiting for transfers between devices, swap(): return lax.ppermute(x, 'blk', [(i, i ^ 1 << bit) for i in range(count)])  55 us
    ppermute x30, starting transfers between devices, swap(): return lax.ppermute(x, 'blk', [(i, i ^ 1 << bit) for i in range(count)])  34.3 us
    dot_general x1, matrix products, on_device(): jnp.einsum('hrl,tl->hrt', q_all, keys, precision=hp, preferred_element_ty...  11.2 us
    convert_element_type x2, other arithmetic, halves(): return (high.astype(jnp.bfloat16), (x - high).astype(jnp.bfloat16))  10.5 us
    dot_general x8, matrix products, dot(): left = jnp.dot(twice, both, preferred_element_type=jnp.float32)  9.1 us
    another operation x16, other arithmetic, gather(): held = jnp.stack([first, second], axis=1).reshape((-1,) + part.shape)  8.79 us
    unnamed x28, local copies, waits for them, and re-layouts  7.82 us
    dot_general x1, matrix products, on_device(): jnp.einsum('hrt,tl->hrl', expo, latent, precision=hp, preferred_element_t...  7.19 us
  transfers between devices with their start and end apart: 30, of which 19 were waited for; matrix products, arithmetic and copies ran while one was open for 22% of the time, Pallas kernels for 0%

commit v1 on v0

--- a/solution.py
+++ b/solution.py
@@ -19,27 +19,21 @@
 def bit_orders(count):
     bits = list(range(1, count.bit_length() - 1))
     low, high = bits[:2], bits[2:][::-1]
-    return low + high, low[::-1] + high
+    return low + high, low[::-1] + high, high + low
 
 
 def gather(block, me, count):
     rows = block.shape[0]
-    parts = []
-    for part, order in zip(jnp.split(block, 2, axis=0), bit_orders(count)):
-        held, bits = part[None], []
-        for bit in order[::-1] + [0]:
-            other = swap(held, bit, count)
-            mine = (me >> bit) & 1
-            place = sum(1 for b in bits if b > bit)
-            shape = (1 << place, -1) + part.shape
-            a, b = held.reshape(shape), other.reshape(shape)
-            first = jnp.where(mine == 0, a, b)
-            second = jnp.where(mine == 0, b, a)
-            held = jnp.stack([first, second], axis=1).reshape((-1,) + part.shape)
-            bits.append(bit)
+    half = rows // 2
+    parts, slots = [], []
+    for c, part in enumerate((block[:half], block[half:])):
+        held, device = part, me[None]
+        for bit in bit_orders(count)[c][::-1] + [0]:
+            held = jnp.concatenate([held, swap(held, bit, count)], axis=0)
+            device = jnp.concatenate([device, device ^ (1 << bit)])
         parts.append(held)
-    whole = jnp.stack(parts, axis=1)
-    return whole.reshape(count * rows, block.shape[1])
+        slots.append((device[:, None] * rows + c * half + jnp.arange(half, dtype=jnp.int32)).reshape(-1))
+    return jnp.concatenate(parts, axis=0), jnp.concatenate(slots)
 
 
 def halves(x):
@@ -48,8 +42,11 @@
 
 
 def split_weight(weight):
-    width = weight.shape[1] // CHUNKS
-    return [jnp.concatenate(halves(weight[:, c * width:(c + 1) * width]), axis=0) for c in range(CHUNKS)]
+    tiles = weight.shape[1] // 128
+    first = tiles // 7
+    step = (tiles - first) // CHUNKS
+    ends = [0] + [(first + c * step) * 128 for c in range(CHUNKS)] + [weight.shape[1]]
+    return [jnp.concatenate(halves(weight[:, i:j]), axis=0) for i, j in zip(ends[:-1], ends[1:])]
 
 
 def project_and_scatter(flat, weights, me, count):
@@ -70,22 +67,30 @@
         left = jnp.dot(twice, both, preferred_element_type=jnp.float32)
         return left + jnp.dot(low, both[:depth], preferred_element_type=jnp.float32)
 
-    orders = bit_orders(count)
-    outs = []
+    paired = []
     for c, both in enumerate(weights):
-        width = both.shape[1]
+        if c >= 2:
+            split, paired[c - 2] = lax.optimization_barrier((split, paired[c - 2]))
         sent = dot(*split[:2], both)
         kept = dot(*split[2:], both)
+        got = swap(sent, 0, count)
         split, kept = lax.optimization_barrier((split, kept))
-        left = kept + swap(sent, 0, count)
+        paired.append(kept + got)
+    first, second, third = bit_orders(count)
+    outs = []
+    for c, left in enumerate(paired):
+        width = left.shape[1]
         bits = list(range(1, count.bit_length() - 1))
-        for bit in orders[c % 2]:
+        for bit in third if c == 0 else (first, second)[c % 2]:
             place = sum(1 for b in bits if b > bit)
             view = left.reshape(1 << place, 2, -1, own, width)
             mine = (me >> bit) & 1
             go = lax.dynamic_index_in_dim(view, 1 - mine, 1, keepdims=False).reshape(-1, width)
             stay = lax.dynamic_index_in_dim(view, mine, 1, keepdims=False).reshape(-1, width)
-            left = stay + swap(go, bit, count)
+            got = swap(go, bit, count)
+            if len(bits) == count.bit_length() - 2:
+                got = lax.optimization_barrier((got, *paired[3:]))[0]
+            left = stay + got
             bits.remove(bit)
         outs.append(left)
     return jnp.concatenate(outs, axis=1)
@@ -100,7 +105,7 @@
     width = queries.shape[1] // heads
     block = jnp.concatenate([cache, owner.astype(f32)[:, None]], axis=1)
     weights = split_weight(out_weight)
-    slab = gather(block, me, count)
+    slab, ids = gather(block, me, count)
     slots = slab.shape[0]
     keys = slab[:, :cache.shape[1]]
     latent = slab[:, :LATENT]
@@ -110,18 +115,12 @@
     q_latent = jnp.einsum("rhn,hln->hrl", q3[:, :, :NOPE], key_up, precision=hp, preferred_element_type=f32)
     q_all = jnp.concatenate([q_latent, jnp.transpose(q3[:, :, NOPE:], (1, 0, 2))], axis=2)
 
-    lanes = math.gcd(slots, 128)
     req_ids = jnp.arange(REQS, dtype=jnp.int32)
     mine = owners[None, :] == req_ids[:, None]
-    ones = mine.astype(f32).reshape(REQS, slots // lanes, lanes)
-    lane = jnp.arange(lanes)
-    before = (lane[:, None] < lane[None, :]).astype(f32)
-    inside = jnp.einsum("rbl,lm->rbm", ones, before, precision=hp, preferred_element_type=f32)
-    row = jnp.arange(slots // lanes)
-    sums = jnp.sum(ones, axis=2)
-    ahead = jnp.sum(jnp.where(row[None, None, :] < row[None, :, None], sums[:, None, :], 0.0), axis=2)
-    position = (inside + ahead[:, :, None]).reshape(REQS, slots).astype(jnp.int32)
-    rel = jnp.where(mine, position - prefix_len[:, None], jnp.int32(2**30))
+    rank = owners * slots + ids
+    below = jnp.sum((rank[:, None] < rank[None, :]).astype(jnp.int32), axis=0)
+    start = jnp.sum((owners[None, :] < req_ids[:, None]).astype(jnp.int32), axis=1)
+    rel = jnp.where(mine, below[None, :] - start[:, None] - prefix_len[:, None], jnp.int32(2**30))
     offset = jnp.arange(SPAN, dtype=jnp.int32)
     visible = (rel[:, None, :] <= offset[None, :, None]).reshape(1, rows, slots)
 

time: 166 us -> 195 us (1.17)
  waiting for transfers between devices: 55 us -> 73.9 us
  local copies, waits for them, and re-layouts: 13.1 us -> 24.4 us
  other arithmetic: 28.5 us -> 23.3 us
  matrix products: 34.2 us -> 36.3 us
    ppermute x30 -> x35, waiting for transfers between devices: 55 us -> 73.9 us  [swap(): return lax.ppermute(x, 'blk', [(i, i ^ 1 << bit) for i in range(count)])]
    concatenate x0 -> x7, local copies, waits for them, and re-layouts: none -> 12.8 us  [the longest x1 6.45 us: gather(): return (jnp.concatenate(parts, axis=0), jnp.concatenate(slots))]
    another operation x19 -> x0, other arithmetic: 9.18 us -> none  [the longest x16 8.79 us: gather(): held = jnp.stack([first, second], axis=1).reshape((-1,) + part.shape)]
    another operation x5 -> x0, local copies, waits for them, and re-layouts: 3.26 us -> none  [the longest x4 2.79 us: gather(): held = jnp.stack([first, second], axis=1).reshape((-1,) + part.shape)]
    concatenate x0 -> x7, other arithmetic: none -> 2.47 us  [the longest x6 2.33 us: gather(): held = jnp.concatenate([held, swap(held, bit, count)], axis=0)]
    dot_general x1, matrix products: 11.2 us -> 13.6 us  [on_device(): jnp.einsum('hrl,tl->hrt', q_all, keys, precision=hp, preferred_element_ty...]
    convert_element_type x2 -> x3, other arithmetic: 10.5 us -> 11.9 us  [halves(): return (high.astype(jnp.bfloat16), (x - high).astype(jnp.bfloat16))]
    ppermute x30 -> x35, starting transfers between devices: 34.3 us -> 35.1 us  [swap(): return lax.ppermute(x, 'blk', [(i, i ^ 1 << bit) for i in range(count)])]
  transfers between devices with their start and end apart: 30 -> 35, of which waited for: 19 -> 17; matrix products, arithmetic and copies ran while one was open for 22% -> 20% of each run, Pallas kernels for 0% -> 0%
where the time goes in v1:
time: 195 us; the launch traced here: 194 us
  waiting for transfers between devices  73.9 us (38%)
  matrix products  36.3 us (19%)
  starting transfers between devices  35.1 us (18%)
  local copies, waits for them, and re-layouts  24.4 us (13%)
  other arithmetic  23.3 us (12%)
    ppermute x35, waiting for transfers between devices, swap(): return lax.ppermute(x, 'blk', [(i, i ^ 1 << bit) for i in range(count)])  73.9 us
    ppermute x35, starting transfers between devices, swap(): return lax.ppermute(x, 'blk', [(i, i ^ 1 << bit) for i in range(count)])  35.1 us
    dot_general x1, matrix products, on_device(): jnp.einsum('hrl,tl->hrt', q_all, keys, precision=hp, preferred_element_ty...  13.6 us
    convert_element_type x3, other arithmetic, halves(): return (high.astype(jnp.bfloat16), (x - high).astype(jnp.bfloat16))  11.9 us
    dot_general x10, matrix products, dot(): left = jnp.dot(twice, both, preferred_element_type=jnp.float32)  8.45 us
    unnamed x45, local copies, waits for them, and re-layouts  7.42 us
    dot_general x1, matrix products, on_device(): jnp.einsum('hrt,tl->hrl', expo, latent, precision=hp, preferred_element_t...  7.2 us
    concatenate x1, local copies, waits for them, and re-layouts, gather(): return (jnp.concatenate(parts, axis=0), jnp.concatenate(slots))  6.45 us
  transfers between devices with their start and end apart: 35, of which 17 were waited for; matrix products, arithmetic and copies ran while one was open for 20% of the time, Pallas kernels for 0%

profile of v1, /device:TPU:0, one launch (start us, length us, event | category | flops | bytes accessed | tf_op | source)
XLA Modules:
  0.0 193.8 jit_solution(9667218409206253024)
XLA Ops:
  0.0 1.2 copy.17
  2.0 3.1 %collective-permute-start.5 = (f32[32,577]{0,1:T(8,128)S(1)}, f32[32,577]{0,1:T(8,128)S(1)}, u32[]{:S(2)}, u32[]{:S(2)}) collective-permute-start(f32[32,577]{0,1:T(8,128)S(1)} %get-tuple-element.109), channel_id=1, source_target_pairs={{0,8},{1,9},{2,10},{3,11},{4,12},{5,13},{6,14},{7,15},{8,0},{9,1},... | collective-permute-start | bytes 221576 | tf_op jit(solution)/shard_map/ppermute | solution.py:16
  5.5 1.4 copy.18
  7.8 2.4 %fusion.24 = f32[4,256,512]{2,1,0:T(8,128)} fusion(f32[4,512,128]{2,1,0:T(8,128)S(1)} %copy-done, f32[256,4,192]{0,2,1:T(8,128)S(1)} %bitcast.182), kind=kOutput, calls=%fused_computation.55 | convolution fusion | flops 402653184 | bytes 3670016 | tf_op jit(solution)/shard_map/rhn,hln->hrl/dot_general | solution.py:115
  10.4 2.6 %collective-permute-done.5 = f32[32,577]{0,1:T(8,128)S(1)} collective-permute-done((f32[32,577]{0,1:T(8,128)S(1)}, f32[32,577]{0,1:T(8,128)S(1)}, u32[]{:S(2)}, u32[]{:S(2)}) %collective-permute-start.5) | collective-permute-done | bytes 73888 | tf_op jit(solution)/shard_map/ppermute | solution.py:16
  13.1 3.1 %collective-permute-start.6 = (f32[64,577]{0,1:T(8,128)S(1)}, f32[64,577]{0,1:T(8,128)S(1)}, u32[]{:S(2)}, u32[]{:S(2)}) collective-permute-start(f32[64,577]{0,1:T(8,128)S(1)} %pad_maximum_fusion.20), channel_id=1, source_target_pairs={{0,16},{1,17},{2,18},{3,19},{4,20},{5,21},{6,22},{7,23},{8,24},{9,... | collective-permute-start | bytes 443144 | tf_op jit(solution)/shard_map/ppermute | solution.py:16
  16.3 8.0 %collective-permute-done = f32[32,577]{0,1:T(8,128)S(1)} collective-permute-done((f32[32,577]{0,1:T(8,128)S(1)}, f32[32,577]{0,1:T(8,128)S(1)}, u32[]{:S(2)}, u32[]{:S(2)}) %collective-permute-start) | collective-permute-done | bytes 73888 | tf_op jit(solution)/shard_map/ppermute | solution.py:16
  24.6 10.5 %collective-permute-done.6 = f32[64,577]{0,1:T(8,128)S(1)} collective-permute-done((f32[64,577]{0,1:T(8,128)S(1)}, f32[64,577]{0,1:T(8,128)S(1)}, u32[]{:S(2)}, u32[]{:S(2)}) %collective-permute-start.6) | collective-permute-done | bytes 147744 | tf_op jit(solution)/shard_map/ppermute | solution.py:16
  35.3 1.2 collective-permute-start.7
  36.6 4.2 %collective-permute-done.1 = f32[64,577]{0,1:T(8,128)S(1)} collective-permute-done((f32[64,577]{0,1:T(8,128)S(1)}, f32[64,577]{0,1:T(8,128)S(1)}, u32[]{:S(2)}, u32[]{:S(2)}) %collective-permute-start.1) | collective-permute-done | bytes 147744 | tf_op jit(solution)/shard_map/ppermute | solution.py:16
  41.1 1.4 collective-permute-start.2
  43.8 7.3 %collective-permute-done.2 = f32[128,577]{0,1:T(8,128)S(1)} collective-permute-done((f32[128,577]{0,1:T(8,128)S(1)}, f32[128,577]{0,1:T(8,128)S(1)}, u32[]{:S(2)}, u32[]{:S(2)}) %collective-permute-start.2) | collective-permute-done | bytes 295456 | tf_op jit(solution)/shard_map/ppermute | solution.py:16
  51.2 1.2 pad_maximum_fusion.15
  52.4 1.3 collective-permute-start.3
  53.8 3.0 %reduce-precision_convert_fusion.4 = (bf16[512,1024]{1,0:T(8,128)(2,1)S(1)}, bf16[512,1024]{1,0:T(8,128)(2,1)}) fusion(f32[512,7168]{1,0:T(8,128)} %param.13), kind=kLoop, calls=%fused_computation.28 | loop fusion | flops 2097152 | bytes 4194304 | tf_op jit(solution)/shard_map/convert_element_type | solution.py:41
  56.8 5.7 %collective-permute-done.8 = f32[256,577]{0,1:T(8,128)} collective-permute-done((f32[256,577]{0,1:T(8,128)S(1)}, f32[256,577]{0,1:T(8,128)}, u32[]{:S(2)}, u32[]{:S(2)}) %collective-permute-start.8) | collective-permute-done | bytes 590880 | tf_op jit(solution)/shard_map/ppermute | solution.py:16
  62.5 3.1 %concatenate.141 = f32[512,577]{0,1:T(8,128)} concatenate(f32[32,577]{0,1:T(8,128)S(1)} %get-tuple-element.109, f32[32,577]{0,1:T(8,128)S(1)} %collective-permute-done.5, f32[64,577]{0,1:T(8,128)S(1)} %collective-permute-done.6, f32[128,577]{0,1:T(8,128)S(1)} %collective-permute-done.7, f32[256,577]{0,1:T(8,128)} %collective-permute-done.8), dimensions={0} | concatenate | bytes 2363392 | tf_op jit(solution)/shard_map/concatenate | solution.py:32
  65.6 2.9 %concatenate.137 = f32[512,577]{0,1:T(8,128)} concatenate(f32[32,577]{0,1:T(8,128)S(1)} %get-tuple-element.110, f32[32,577]{0,1:T(8,128)S(1)} %collective-permute-done, f32[64,577]{0,1:T(8,128)S(1)} %collective-permute-done.1, f32[128,577]{0,1:T(8,128)S(1)} %collective-permute-done.2, f32[256,577]{0,1:T(8,128)} %collective-permute-done.3), dimensions={0} | concatenate | bytes 2363392 | tf_op jit(solution)/shard_map/concatenate | solution.py:32
  71.5 8.8 %fusion.9 = (bf16[512,1536]{1,0:T(8,128)(2,1)}, bf16[512,1536]{1,0:T(8,128)(2,1)}, bf16[512,1536]{1,0:T(8,128)(2,1)}, bf16[512,1536]{1,0:T(8,128)(2,1)}, bf16[51...) fusion(f32[512,7168]{1,0:T(8,128)} %param.13), kind=kLoop, calls=%fused_computation.22 | loop fusion | flops 12582912 | bytes 25165824 | tf_op jit(solution)/shard_map/convert_element_type | solution.py:41
  80.3 6.5 %concatenate.142 = f32[2048,577]{0,1:T(8,128)} concatenate(f32[32,577]{0,1:T(8,128)S(1)} %get-tuple-element.110, f32[32,577]{0,1:T(8,128)} %copy-done.5, f32[64,577]{0,1:T(8,128)} %copy-done.7, f32[128,577]{0,1:T(8,128)} %copy-done.10, f32[256,577]{0,1:T(8,128)} %collective-permute-done.3, f32[512,577]{0,1:T(8,128)} %collective-permute-done.4, f32[32,577]{0,1:T(8,128)S(1)} %get-tuple-element.109, ...), dimensions={0} | concatenate | bytes 9453568 | tf_op jit(solution)/shard_map/concatenate | solution.py:36
  88.6 1.7 convert_reduce_fusion
  90.8 13.6 %select_reduce_fusion = (f32[4,256]{1,0:T(4,128)S(1)}, f32[4,256,2048]{2,1,0:T(8,128)S(1)}) fusion(pred[256,2048]{1,0:T(8,128)(4,1)S(1)} %broadcast_compare_fusion, f32[2048,577]{0,1:T(8,128)} %concatenate.142, f32[4,256,64]{2,1,0:T(8,128)} %bitcast.210, f32[4,256,512]{2,1,0:T(8,128)} %fusion.24), kind=kOutput, calls=%fused_computation.2 | convolution fusion | flops 7252540416 | bytes 16257024 | tf_op jit(solution)/shard_map/hrl,tl->hrt/dot_general | solution.py:127
  104.4 2.2 %fusion = f32[4,256]{1,0:T(4,128)S(1)} fusion(f32[4,256,2048]{2,1,0:T(8,128)S(1)} %get-tuple-element.112, f32[4,256]{1,0:T(4,128)S(1)} %get-tuple-element.111, pred[256,2048]{1,0:T(8,128)(4,1)S(1)} %broadcast_compare_fusion), kind=kLoop, calls=%fused_computation.3 | loop fusion | flops 6290432 | bytes 8921088 | tf_op jit(solution)/shard_map/reduce_sum | solution.py:131
  106.7 7.2 %fusion.1 = f32[4,256,512]{2,1,0:T(8,128)S(1)} fusion(f32[4,256,2048]{2,1,0:T(8,128)S(1)} %get-tuple-element.112, f32[2048,577]{0,1:T(8,128)S(1)} %bitcast.181, f32[4,256]{1,0:T(4,128)S(1)} %get-tuple-element.111, pred[256,2048]{1,0:T(8,128)(4,1)S(1)} %broadcast_compare_fusion), kind=kOutput, calls=%fused_computation.4 | convolution fusion | flops 6446645248 | bytes 15208448 | tf_op jit(solution)/shard_map/hrt,tl->hrl/dot_general | solution.py:132
  115.0 1.1 copy.23
  116.1 1.3 reshape_reshape.3
  117.4 1.7 fusion.18
  131.5 1.6 collective-permute-start.19
  136.7 1.6 collective-permute-start.23
  139.0 12.0 %collective-permute-done.27 = f32[64,1536]{1,0:T(8,128)S(1)} collective-permute-done((f32[64,1536]{1,0:T(8,128)S(1)}, f32[64,1536]{1,0:T(8,128)S(1)}, u32[]{:S(2)}, u32[]{:S(2)}) %collective-permute-start.27) | collective-permute-done | bytes 393248 | tf_op jit(solution)/shard_map/ppermute | solution.py:16
  151.1 1.5 collective-permute-start.28
  152.7 1.6 collective-permute-start.24
  154.4 1.1 collective-permute-start.16
  156.2 3.2 %collective-permute-done.16 = f32[32,1024]{1,0:T(8,128)S(1)} collective-permute-done((f32[32,1024]{1,0:T(8,128)S(1)}, f32[32,1024]{1,0:T(8,128)S(1)}, u32[]{:S(2)}, u32[]{:S(2)}) %collective-permute-start.16) | collective-permute-done | bytes 131104 | tf_op jit(solution)/shard_map/ppermute | solution.py:16
  160.1 1.2 collective-permute-done.28
  161.4 2.2 %collective-permute-start.29 = (f32[16,1536]{1,0:T(8,128)S(1)}, f32[16,1536]{1,0:T(8,128)S(1)}, u32[]{:S(2)}, u32[]{:S(2)}) collective-permute-start(f32[16,1536]{1,0:T(8,128)S(1)} %dynamic-slice_bitcast_fusion.9), channel_id=1, source_target_pairs={{0,16},{1,17},{2,18},{3,19},{4,20},{5,21},{6,22},{7,23},{8,24},{9,... | collective-permute-start | bytes 294920 | tf_op jit(solution)/shard_map/ppermute | solution.py:16
  164.5 1.7 collective-permute-done.17
  166.3 1.3 collective-permute-start.18
  167.6 1.9 collective-permute-start.21
  171.2 3.3 %collective-permute-done.25 = f32[16,1536]{1,0:T(8,128)S(1)} collective-permute-done((f32[16,1536]{1,0:T(8,128)S(1)}, f32[16,1536]{1,0:T(8,128)S(1)}, u32[]{:S(2)}, u32[]{:S(2)}) %collective-permute-start.25) | collective-permute-done | bytes 98336 | tf_op jit(solution)/shard_map/ppermute | solution.py:16
  174.6 1.7 collective-permute-done.21
  176.8 1.4 collective-permute-start.32
  178.1 2.4 %collective-permute-done.22 = f32[8,1536]{1,0:T(8,128)S(1)} collective-permute-done((f32[8,1536]{1,0:T(8,128)S(1)}, f32[8,1536]{1,0:T(8,128)S(1)}, u32[]{:S(2)}, u32[]{:S(2)}) %collective-permute-start.22) | collective-permute-done | bytes 49184 | tf_op jit(solution)/shard_map/ppermute | solution.py:16
  180.5 2.7 %collective-permute-done.32 = f32[32,1536]{1,0:T(8,128)S(1)} collective-permute-done((f32[32,1536]{1,0:T(8,128)S(1)}, f32[32,1536]{1,0:T(8,128)S(1)}, u32[]{:S(2)}, u32[]{:S(2)}) %collective-permute-start.32) | collective-permute-done | bytes 196640 | tf_op jit(solution)/shard_map/ppermute | solution.py:16
  183.2 1.1 collective-permute-start.33
  184.4 4.4 %collective-permute-done.33 = f32[16,1536]{1,0:T(8,128)S(1)} collective-permute-done((f32[16,1536]{1,0:T(8,128)S(1)}, f32[16,1536]{1,0:T(8,128)S(1)}, u32[]{:S(2)}, u32[]{:S(2)}) %collective-permute-start.33) | collective-permute-done | bytes 98336 | tf_op jit(solution)/shard_map/ppermute | solution.py:16
  188.8 2.3 %collective-permute-start.34 = (f32[8,1536]{1,0:T(8,128)S(1)}, f32[8,1536]{1,0:T(8,128)S(1)}, u32[]{:S(2)}, u32[]{:S(2)}) collective-permute-start(f32[8,1536]{1,0:T(8,128)S(1)} %dynamic-slice_bitcast_fusion.13), channel_id=1, source_target_pairs={{0,8},{1,9},{2,10},{3,11},{4,12},{5,13},{6,14},{7,15},{8,0},{9,1},... | collective-permute-start | bytes 147464 | tf_op jit(solution)/shard_map/ppermute | solution.py:16
  191.2 2.0 %collective-permute-done.34 = f32[8,1536]{1,0:T(8,128)S(1)} collective-permute-done((f32[8,1536]{1,0:T(8,128)S(1)}, f32[8,1536]{1,0:T(8,128)S(1)}, u32[]{:S(2)}, u32[]{:S(2)}) %collective-permute-start.34) | collective-permute-done | bytes 49184 | tf_op jit(solution)/shard_map/ppermute | solution.py:16
  (184 shorter events, 32.8 us)
Async XLA Ops:
  0.0 7.8 %copy-start = (f32[4,512,128]{2,1,0:T(8,128)S(1)}, f32[4,512,128]{2,1,0:T(8,128)}, u32[]{:S(2)}) copy-start(f32[4,512,128]{2,1,0:T(8,128)} %param.11) | copy-start | bytes 3145732
  2.0 11.0 %collective-permute-start.5 = (f32[32,577]{0,1:T(8,128)S(1)}, f32[32,577]{0,1:T(8,128)S(1)}, u32[]{:S(2)}, u32[]{:S(2)}) collective-permute-start(f32[32,577]{0,1:T(8,128)S(1)} %get-tuple-element.109), channel_id=1, source_target_pairs={{0,8},{1,9},{2,10},{3,11},{4,12},{5,13},{6,14},{7,15},{8,0},{9,1},... | collective-permute-start | bytes 221576 | tf_op jit(solution)/shard_map/ppermute | solution.py:16
  5.1 19.2 %collective-permute-start = (f32[32,577]{0,1:T(8,128)S(1)}, f32[32,577]{0,1:T(8,128)S(1)}, u32[]{:S(2)}, u32[]{:S(2)}) collective-permute-start(f32[32,577]{0,1:T(8,128)S(1)} %get-tuple-element.110), channel_id=1, source_target_pairs={{0,8},{1,9},{2,10},{3,11},{4,12},{5,13},{6,14},{7,15},{8,0},{9,1},... | collective-permute-start | bytes 221576 | tf_op jit(solution)/shard_map/ppermute | solution.py:16
  13.1 22.0 %collective-permute-start.6 = (f32[64,577]{0,1:T(8,128)S(1)}, f32[64,577]{0,1:T(8,128)S(1)}, u32[]{:S(2)}, u32[]{:S(2)}) collective-permute-start(f32[64,577]{0,1:T(8,128)S(1)} %pad_maximum_fusion.20), channel_id=1, source_target_pairs={{0,16},{1,17},{2,18},{3,19},{4,20},{5,21},{6,22},{7,23},{8,24},{9,... | collective-permute-start | bytes 443144 | tf_op jit(solution)/shard_map/ppermute | solution.py:16
  24.2 41.4 %copy-start.5 = (f32[32,577]{0,1:T(8,128)}, f32[32,577]{0,1:T(8,128)S(1)}, u32[]{:S(2)}) copy-start(f32[32,577]{0,1:T(8,128)S(1)} %collective-permute-done) | copy-start | bytes 221572
  24.4 16.4 %collective-permute-start.1 = (f32[64,577]{0,1:T(8,128)S(1)}, f32[64,577]{0,1:T(8,128)S(1)}, u32[]{:S(2)}, u32[]{:S(2)}) collective-permute-start(f32[64,577]{0,1:T(8,128)S(1)} %pad_maximum_fusion.18), channel_id=1, source_target_pairs={{0,16},{1,17},{2,18},{3,19},{4,20},{5,21},{6,22},{7,23},{8,24},{9,... | collective-permute-start | bytes 443144 | tf_op jit(solution)/shard_map/ppermute | solution.py:16
  35.1 27.4 %copy-start.6 = (f32[64,577]{0,1:T(8,128)}, f32[64,577]{0,1:T(8,128)S(1)}, u32[]{:S(2)}) copy-start(f32[64,577]{0,1:T(8,128)S(1)} %collective-permute-done.6) | copy-start | bytes 443140
  35.3 7.2 %collective-permute-start.7 = (f32[128,577]{0,1:T(8,128)S(1)}, f32[128,577]{0,1:T(8,128)S(1)}, u32[]{:S(2)}, u32[]{:S(2)}) collective-permute-start(f32[128,577]{0,1:T(8,128)S(1)} %pad_maximum_fusion.21), channel_id=1, source_target_pairs={{0,2},{1,3},{2,0},{3,1},{4,6},{5,7},{6,4},{7,5},{8,10},{9,11},{10,... | collective-permute-start | bytes 886280 | tf_op jit(solution)/shard_map/ppermute | solution.py:16
  40.8 24.8 %copy-start.7 = (f32[64,577]{0,1:T(8,128)}, f32[64,577]{0,1:T(8,128)S(1)}, u32[]{:S(2)}) copy-start(f32[64,577]{0,1:T(8,128)S(1)} %collective-permute-done.1) | copy-start | bytes 443140
  41.1 10.1 %collective-permute-start.2 = (f32[128,577]{0,1:T(8,128)S(1)}, f32[128,577]{0,1:T(8,128)S(1)}, u32[]{:S(2)}, u32[]{:S(2)}) collective-permute-start(f32[128,577]{0,1:T(8,128)S(1)} %pad_maximum_fusion.19), channel_id=1, source_target_pairs={{0,4},{1,5},{2,6},{3,7},{4,0},{5,1},{6,2},{7,3},{8,12},{9,13},{10,... | collective-permute-start | bytes 886280 | tf_op jit(solution)/shard_map/ppermute | solution.py:16
  42.5 20.0 %copy-start.9 = (f32[128,577]{0,1:T(8,128)}, f32[128,577]{0,1:T(8,128)S(1)}, u32[]{:S(2)}) copy-start(f32[128,577]{0,1:T(8,128)S(1)} %collective-permute-done.7) | copy-start | bytes 886276
  42.9 19.6 %collective-permute-start.8 = (f32[256,577]{0,1:T(8,128)S(1)}, f32[256,577]{0,1:T(8,128)}, u32[]{:S(2)}, u32[]{:S(2)}) collective-permute-start(f32[256,577]{0,1:T(8,128)S(1)} %pad_maximum_fusion.16), channel_id=1, source_target_pairs={{0,4},{1,5},{2,6},{3,7},{4,0},{5,1},{6,2},{7,3},{8,12},{9,13},{10,... | collective-permute-start | bytes 1772552 | tf_op jit(solution)/shard_map/ppermute | solution.py:16
  51.1 14.5 %copy-start.10 = (f32[128,577]{0,1:T(8,128)}, f32[128,577]{0,1:T(8,128)S(1)}, u32[]{:S(2)}) copy-start(f32[128,577]{0,1:T(8,128)S(1)} %collective-permute-done.2) | copy-start | bytes 886276
  52.4 13.2 %collective-permute-start.3 = (f32[256,577]{0,1:T(8,128)}, f32[256,577]{0,1:T(8,128)}, u32[]{:S(2)}, u32[]{:S(2)}) collective-permute-start(f32[256,577]{0,1:T(8,128)} %pad_maximum_fusion.15), channel_id=1, source_target_pairs={{0,2},{1,3},{2,0},{3,1},{4,6},{5,7},{6,4},{7,5},{8,10},{9,11},{10,... | collective-permute-start | bytes 1772552 | tf_op jit(solution)/shard_map/ppermute | solution.py:16
  65.6 14.7 %collective-permute-start.9 = (f32[512,577]{0,1:T(8,128)}, f32[512,577]{0,1:T(8,128)}, u32[]{:S(2)}, u32[]{:S(2)}) collective-permute-start(f32[512,577]{0,1:T(8,128)} %concatenate.141), channel_id=1, source_target_pairs={{0,1},{1,0},{2,3},{3,2},{4,5},{5,4},{6,7},{7,6},{8,9},{9,8},{10,11... | collective-permute-start | bytes 3545096 | tf_op jit(solution)/shard_map/ppermute | solution.py:16
  68.6 11.7 %collective-permute-start.4 = (f32[512,577]{0,1:T(8,128)}, f32[512,577]{0,1:T(8,128)}, u32[]{:S(2)}, u32[]{:S(2)}) collective-permute-start(f32[512,577]{0,1:T(8,128)} %concatenate.137), channel_id=1, source_target_pairs={{0,1},{1,0},{2,3},{3,2},{4,5},{5,4},{6,7},{7,6},{8,9},{9,8},{10,11... | collective-permute-start | bytes 3545096 | tf_op jit(solution)/shard_map/ppermute | solution.py:16
  80.3 10.0 %copy-start.17 = (s32[2]{0:T(128)S(1)}, s32[2]{0:T(128)}, u32[]{:S(2)}) copy-start(s32[2]{0:T(128)} %param.10) | copy-start | bytes 28
  90.4 16.2 %slice-start = ((s8[4784128]{0:T(1024)(128)(4,1)}), s8[4194304]{0:T(1024)(128)(4,1)S(1)}, s32[]{:S(2)}) async-start(s8[4784128]{0:T(1024)(128)(4,1)} %bitcast.180), calls=%async_computation | async-start | bytes 8388608
  90.8 15.9 %slice-start.1 = ((s8[4784128]{0:T(1024)(128)(4,1)}), s8[589824]{0:T(1024)(128)(4,1)S(1)}, s32[]{:S(2)}) async-start(s8[4784128]{0:T(1024)(128)(4,1)} %bitcast.180), calls=%async_computation.1 | async-start | bytes 1179648
  106.7 7.2 %copy-start.18 = (f32[4,512,128]{2,1,0:T(8,128)S(1)}, f32[4,512,128]{2,1,0:T(8,128)}, u32[]{:S(2)}) copy-start(f32[4,512,128]{2,1,0:T(8,128)} %param.12) | copy-start | bytes 3145732
  120.1 3.6 %collective-permute-start.10 = (f32[128,1024]{1,0:T(8,128)S(1)}, f32[128,1024]{1,0:T(8,128)S(1)}, u32[]{:S(2)}, u32[]{:S(2)}) collective-permute-start(f32[128,1024]{1,0:T(8,128)S(1)} %convolution_add_fusion.8), channel_id=1, source_target_pairs={{0,1},{1,0},{2,3},{3,2},{4,5},{5,4},{6,7},{7,6},{8,9},{9,8},{10,11... | collective-permute-start | bytes 1572872 | tf_op jit(solution)/shard_map/ppermute | solution.py:16
  123.5 3.9 %collective-permute-start.12 = (f32[128,1536]{1,0:T(8,128)S(1)}, f32[128,1536]{1,0:T(8,128)S(1)}, u32[]{:S(2)}, u32[]{:S(2)}) collective-permute-start(f32[128,1536]{1,0:T(8,128)S(1)} %convolution_add_fusion.5), channel_id=1, source_target_pairs={{0,1},{1,0},{2,3},{3,2},{4,5},{5,4},{6,7},{7,6},{8,9},{9,8},{10,11... | collective-permute-start | bytes 2359304 | tf_op jit(solution)/shard_map/ppermute | solution.py:16
  125.8 7.2 %collective-permute-start.14 = (f32[128,1536]{1,0:T(8,128)S(1)}, f32[128,1536]{1,0:T(8,128)S(1)}, u32[]{:S(2)}, u32[]{:S(2)}) collective-permute-start(f32[128,1536]{1,0:T(8,128)S(1)} %convolution_add_fusion.2), channel_id=1, source_target_pairs={{0,1},{1,0},{2,3},{3,2},{4,5},{5,4},{6,7},{7,6},{8,9},{9,8},{10,11... | collective-permute-start | bytes 2359304 | tf_op jit(solution)/shard_map/ppermute | solution.py:16
  127.4 26.9 %collective-permute-start.11 = (f32[64,1024]{1,0:T(8,128)S(1)}, f32[64,1024]{1,0:T(8,128)S(1)}, u32[]{:S(2)}, u32[]{:S(2)}) collective-permute-start(f32[64,1024]{1,0:T(8,128)S(1)} %dynamic-slice_bitcast_fusion.2), channel_id=1, source_target_pairs={{0,16},{1,17},{2,18},{3,19},{4,20},{5,21},{6,22},{7,23},{8,24},{9,... | collective-permute-start | bytes 786440 | tf_op jit(solution)/shard_map/ppermute | solution.py:16
  130.8 4.8 %collective-permute-start.13 = (f32[128,1536]{1,0:T(8,128)S(1)}, f32[128,1536]{1,0:T(8,128)S(1)}, u32[]{:S(2)}, u32[]{:S(2)}) collective-permute-start(f32[128,1536]{1,0:T(8,128)S(1)} %convolution_add_fusion.3), channel_id=1, source_target_pairs={{0,1},{1,0},{2,3},{3,2},{4,5},{5,4},{6,7},{7,6},{8,9},{9,8},{10,11... | collective-permute-start | bytes 2359304 | tf_op jit(solution)/shard_map/ppermute | solution.py:16
  131.4 2.1 %copy-start.11 = (bf16[512,1536]{1,0:T(8,128)(2,1)S(1)}, bf16[512,1536]{1,0:T(8,128)(2,1)}, u32[]{:S(2)}) copy-start(bf16[512,1536]{1,0:T(8,128)(2,1)} %get-tuple-element.91) | copy-start | bytes 4718596
  131.5 22.9 %collective-permute-start.19 = (f32[64,1536]{1,0:T(8,128)S(1)}, f32[64,1536]{1,0:T(8,128)S(1)}, u32[]{:S(2)}, u32[]{:S(2)}) collective-permute-start(f32[64,1536]{1,0:T(8,128)S(1)} %bitcast.213), channel_id=1, source_target_pairs={{0,4},{1,5},{2,6},{3,7},{4,0},{5,1},{6,2},{7,3},{8,12},{9,13},{10,... | collective-permute-start | bytes 1179656 | tf_op jit(solution)/shard_map/ppermute | solution.py:16
  134.3 3.9 %collective-permute-start.15 = (f32[128,1536]{1,0:T(8,128)S(1)}, f32[128,1536]{1,0:T(8,128)S(1)}, u32[]{:S(2)}, u32[]{:S(2)}) collective-permute-start(f32[128,1536]{1,0:T(8,128)S(1)} %convolution_add_fusion), channel_id=1, source_target_pairs={{0,1},{1,0},{2,3},{3,2},{4,5},{5,4},{6,7},{7,6},{8,9},{9,8},{10,11... | collective-permute-start | bytes 2359304 | tf_op jit(solution)/shard_map/ppermute | solution.py:16
  135.8 15.2 %collective-permute-start.27 = (f32[64,1536]{1,0:T(8,128)S(1)}, f32[64,1536]{1,0:T(8,128)S(1)}, u32[]{:S(2)}, u32[]{:S(2)}) collective-permute-start(f32[64,1536]{1,0:T(8,128)S(1)} %bitcast.214), channel_id=1, source_target_pairs={{0,4},{1,5},{2,6},{3,7},{4,0},{5,1},{6,2},{7,3},{8,12},{9,13},{10,... | collective-permute-start | bytes 1179656 | tf_op jit(solution)/shard_map/ppermute | solution.py:16
  136.7 16.0 %collective-permute-start.23 = (f32[64,1536]{1,0:T(8,128)S(1)}, f32[64,1536]{1,0:T(8,128)S(1)}, u32[]{:S(2)}, u32[]{:S(2)}) collective-permute-start(f32[64,1536]{1,0:T(8,128)S(1)} %dynamic-slice_bitcast_fusion.1), channel_id=1, source_target_pairs={{0,2},{1,3},{2,0},{3,1},{4,6},{5,7},{6,4},{7,5},{8,10},{9,11},{10,... | collective-permute-start | bytes 1179656 | tf_op jit(solution)/shard_map/ppermute | solution.py:16
  138.4 38.3 %collective-permute-start.31 = (f32[64,1536]{1,0:T(8,128)S(1)}, f32[64,1536]{1,0:T(8,128)S(1)}, u32[]{:S(2)}, u32[]{:S(2)}) collective-permute-start(f32[64,1536]{1,0:T(8,128)S(1)} %dynamic-slice_bitcast_fusion), channel_id=1, source_target_pairs={{0,2},{1,3},{2,0},{3,1},{4,6},{5,7},{6,4},{7,5},{8,10},{9,11},{10,... | collective-permute-start | bytes 1179656 | tf_op jit(solution)/shard_map/ppermute | solution.py:16
  151.1 10.2 %collective-permute-start.28 = (f32[32,1536]{1,0:T(8,128)S(1)}, f32[32,1536]{1,0:T(8,128)S(1)}, u32[]{:S(2)}, u32[]{:S(2)}) collective-permute-start(f32[32,1536]{1,0:T(8,128)S(1)} %dynamic-slice_bitcast_fusion.4), channel_id=1, source_target_pairs={{0,2},{1,3},{2,0},{3,1},{4,6},{5,7},{6,4},{7,5},{8,10},{9,11},{10,... | collective-permute-start | bytes 589832 | tf_op jit(solution)/shard_map/ppermute | solution.py:16
  152.7 10.9 %collective-permute-start.24 = (f32[32,1536]{1,0:T(8,128)S(1)}, f32[32,1536]{1,0:T(8,128)S(1)}, u32[]{:S(2)}, u32[]{:S(2)}) collective-permute-start(f32[32,1536]{1,0:T(8,128)S(1)} %dynamic-slice_bitcast_fusion.5), channel_id=1, source_target_pairs={{0,4},{1,5},{2,6},{3,7},{4,0},{5,1},{6,2},{7,3},{8,12},{9,13},{10,... | collective-permute-start | bytes 589832 | tf_op jit(solution)/shard_map/ppermute | solution.py:16
  154.4 5.0 %collective-permute-start.16 = (f32[32,1024]{1,0:T(8,128)S(1)}, f32[32,1024]{1,0:T(8,128)S(1)}, u32[]{:S(2)}, u32[]{:S(2)}) collective-permute-start(f32[32,1024]{1,0:T(8,128)S(1)} %dynamic-slice_bitcast_fusion.7), channel_id=1, source_target_pairs={{0,8},{1,9},{2,10},{3,11},{4,12},{5,13},{6,14},{7,15},{8,0},{9,1},... | collective-permute-start | bytes 393224 | tf_op jit(solution)/shard_map/ppermute | solution.py:16
  155.6 12.0 %collective-permute-start.20 = (f32[32,1536]{1,0:T(8,128)S(1)}, f32[32,1536]{1,0:T(8,128)S(1)}, u32[]{:S(2)}, u32[]{:S(2)}) collective-permute-start(f32[32,1536]{1,0:T(8,128)S(1)} %dynamic-slice_bitcast_fusion.6), channel_id=1, source_target_pairs={{0,2},{1,3},{2,0},{3,1},{4,6},{5,7},{6,4},{7,5},{8,10},{9,11},{10,... | collective-permute-start | bytes 589832 | tf_op jit(solution)/shard_map/ppermute | solution.py:16
  159.5 6.8 %collective-permute-start.17 = (f32[16,1024]{1,0:T(8,128)S(1)}, f32[16,1024]{1,0:T(8,128)S(1)}, u32[]{:S(2)}, u32[]{:S(2)}) collective-permute-start(f32[16,1024]{1,0:T(8,128)S(1)} %dynamic-slice_bitcast_fusion.12), channel_id=1, source_target_pairs={{0,2},{1,3},{2,0},{3,1},{4,6},{5,7},{6,4},{7,5},{8,10},{9,11},{10,... | collective-permute-start | bytes 196616 | tf_op jit(solution)/shard_map/ppermute | solution.py:16
  161.4 32.5 %copy-start.1 = (f32[4,512,128]{2,1,0:T(8,128)S(1)}, f32[4,512,128]{2,1,0:T(8,128)}, u32[]{:S(2)}) copy-start(f32[4,512,128]{2,1,0:T(8,128)} %param.11) | copy-start | bytes 3145732
  161.4 8.9 %collective-permute-start.29 = (f32[16,1536]{1,0:T(8,128)S(1)}, f32[16,1536]{1,0:T(8,128)S(1)}, u32[]{:S(2)}, u32[]{:S(2)}) collective-permute-start(f32[16,1536]{1,0:T(8,128)S(1)} %dynamic-slice_bitcast_fusion.9), channel_id=1, source_target_pairs={{0,16},{1,17},{2,18},{3,19},{4,20},{5,21},{6,22},{7,23},{8,24},{9,... | collective-permute-start | bytes 294920 | tf_op jit(solution)/shard_map/ppermute | solution.py:16
  163.7 10.8 %collective-permute-start.25 = (f32[16,1536]{1,0:T(8,128)S(1)}, f32[16,1536]{1,0:T(8,128)S(1)}, u32[]{:S(2)}, u32[]{:S(2)}) collective-permute-start(f32[16,1536]{1,0:T(8,128)S(1)} %dynamic-slice_bitcast_fusion.10), channel_id=1, source_target_pairs={{0,16},{1,17},{2,18},{3,19},{4,20},{5,21},{6,22},{7,23},{8,24},{9,... | collective-permute-start | bytes 294920 | tf_op jit(solution)/shard_map/ppermute | solution.py:16
  166.3 4.0 %collective-permute-start.18 = (f32[8,1024]{1,0:T(8,128)S(1)}, f32[8,1024]{1,0:T(8,128)S(1)}, u32[]{:S(2)}, u32[]{:S(2)}) collective-permute-start(f32[8,1024]{1,0:T(8,128)S(1)} %dynamic-slice_bitcast_fusion.17), channel_id=1, source_target_pairs={{0,4},{1,5},{2,6},{3,7},{4,0},{5,1},{6,2},{7,3},{8,12},{9,13},{10,... | collective-permute-start | bytes 98312 | tf_op jit(solution)/shard_map/ppermute | solution.py:16
  167.6 8.7 %collective-permute-start.21 = (f32[16,1536]{1,0:T(8,128)S(1)}, f32[16,1536]{1,0:T(8,128)S(1)}, u32[]{:S(2)}, u32[]{:S(2)}) collective-permute-start(f32[16,1536]{1,0:T(8,128)S(1)} %dynamic-slice_bitcast_fusion.11), channel_id=1, source_target_pairs={{0,16},{1,17},{2,18},{3,19},{4,20},{5,21},{6,22},{7,23},{8,24},{9,... | collective-permute-start | bytes 294920 | tf_op jit(solution)/shard_map/ppermute | solution.py:16
  170.3 20.8 %collective-permute-start.30 = (f32[8,1536]{1,0:T(8,128)S(1)}, f32[8,1536]{1,0:T(8,128)S(1)}, u32[]{:S(2)}, u32[]{:S(2)}) collective-permute-start(f32[8,1536]{1,0:T(8,128)S(1)} %dynamic-slice_bitcast_fusion.14), channel_id=1, source_target_pairs={{0,8},{1,9},{2,10},{3,11},{4,12},{5,13},{6,14},{7,15},{8,0},{9,1},... | collective-permute-start | bytes 147464 | tf_op jit(solution)/shard_map/ppermute | solution.py:16
  174.5 9.9 %collective-permute-start.26 = (f32[8,1536]{1,0:T(8,128)S(1)}, f32[8,1536]{1,0:T(8,128)S(1)}, u32[]{:S(2)}, u32[]{:S(2)}) collective-permute-start(f32[8,1536]{1,0:T(8,128)S(1)} %dynamic-slice_bitcast_fusion.15), channel_id=1, source_target_pairs={{0,8},{1,9},{2,10},{3,11},{4,12},{5,13},{6,14},{7,15},{8,0},{9,1},... | collective-permute-start | bytes 147464 | tf_op jit(solution)/shard_map/ppermute | solution.py:16
  176.3 4.2 %collective-permute-start.22 = (f32[8,1536]{1,0:T(8,128)S(1)}, f32[8,1536]{1,0:T(8,128)S(1)}, u32[]{:S(2)}, u32[]{:S(2)}) collective-permute-start(f32[8,1536]{1,0:T(8,128)S(1)} %dynamic-slice_bitcast_fusion.16), channel_id=1, source_target_pairs={{0,8},{1,9},{2,10},{3,11},{4,12},{5,13},{6,14},{7,15},{8,0},{9,1},... | collective-permute-start | bytes 147464 | tf_op jit(solution)/shard_map/ppermute | solution.py:16
  176.8 6.4 %collective-permute-start.32 = (f32[32,1536]{1,0:T(8,128)S(1)}, f32[32,1536]{1,0:T(8,128)S(1)}, u32[]{:S(2)}, u32[]{:S(2)}) collective-permute-start(f32[32,1536]{1,0:T(8,128)S(1)} %dynamic-slice_bitcast_fusion.3), channel_id=1, source_target_pairs={{0,4},{1,5},{2,6},{3,7},{4,0},{5,1},{6,2},{7,3},{8,12},{9,13},{10,... | collective-permute-start | bytes 589832 | tf_op jit(solution)/shard_map/ppermute | solution.py:16
  183.2 5.6 %collective-permute-start.33 = (f32[16,1536]{1,0:T(8,128)S(1)}, f32[16,1536]{1,0:T(8,128)S(1)}, u32[]{:S(2)}, u32[]{:S(2)}) collective-permute-start(f32[16,1536]{1,0:T(8,128)S(1)} %dynamic-slice_bitcast_fusion.8), channel_id=1, source_target_pairs={{0,16},{1,17},{2,18},{3,19},{4,20},{5,21},{6,22},{7,23},{8,24},{9,... | collective-permute-start | bytes 294920 | tf_op jit(solution)/shard_map/ppermute | solution.py:16
  188.8 4.4 %collective-permute-start.34 = (f32[8,1536]{1,0:T(8,128)S(1)}, f32[8,1536]{1,0:T(8,128)S(1)}, u32[]{:S(2)}, u32[]{:S(2)}) collective-permute-start(f32[8,1536]{1,0:T(8,128)S(1)} %dynamic-slice_bitcast_fusion.13), channel_id=1, source_target_pairs={{0,8},{1,9},{2,10},{3,11},{4,12},{5,13},{6,14},{7,15},{8,0},{9,1},... | collective-permute-start | bytes 147464 | tf_op jit(solution)/shard_map/ppermute | solution.py:16
  191.2 2.1 %copy-start.16 = (f32[8,7168]{1,0:T(8,128)}, f32[8,7168]{1,0:T(8,128)S(1)}, u32[]{:S(2)}) copy-start(f32[8,7168]{1,0:T(8,128)S(1)} %fusion.34) | copy-start | bytes 688132
  (8 other events, 12.2 us)

commit v2 on v0

--- a/solution.py
+++ b/solution.py
@@ -71,13 +71,16 @@
         return left + jnp.dot(low, both[:depth], preferred_element_type=jnp.float32)
 
     orders = bit_orders(count)
-    outs = []
+    paired, outs = [], []
     for c, both in enumerate(weights):
-        width = both.shape[1]
+        if c >= 2:
+            split, paired[c - 2] = lax.optimization_barrier((split, paired[c - 2]))
         sent = dot(*split[:2], both)
         kept = dot(*split[2:], both)
         split, kept = lax.optimization_barrier((split, kept))
-        left = kept + swap(sent, 0, count)
+        paired.append(kept + swap(sent, 0, count))
+    for c, left in enumerate(paired):
+        width = left.shape[1]
         bits = list(range(1, count.bit_length() - 1))
         for bit in orders[c % 2]:
             place = sum(1 for b in bits if b > bit)

time: 166 us -> 172 us (1.036)
  waiting for transfers between devices: 55 us -> 69.2 us
  starting transfers between devices: 34.3 us -> 27.1 us
    ppermute x30, waiting for transfers between devices: 55 us -> 69.2 us  [swap(): return lax.ppermute(x, 'blk', [(i, i ^ 1 << bit) for i in range(count)])]
    ppermute x30, starting transfers between devices: 34.3 us -> 27.1 us  [swap(): return lax.ppermute(x, 'blk', [(i, i ^ 1 << bit) for i in range(count)])]
  transfers between devices with their start and end apart: 30 -> 30, of which waited for: 19 -> 21; matrix products, arithmetic and copies ran while one was open for 22% -> 22% of each run, Pallas kernels for 0% -> 0%
where the time goes in v2:
time: 172 us
  waiting for transfers between devices  69.2 us (40%)
  matrix products  34.3 us (20%)
  other arithmetic  28.3 us (16%)
  starting transfers between devices  27.1 us (16%)
  local copies, waits for them, and re-layouts  12.2 us (7%)
    ppermute x30, waiting for transfers between devices, swap(): return lax.ppermute(x, 'blk', [(i, i ^ 1 << bit) for i in range(count)])  69.2 us
    ppermute x30, starting transfers between devices, swap(): return lax.ppermute(x, 'blk', [(i, i ^ 1 << bit) for i in range(count)])  27.1 us
    dot_general x1, matrix products, on_device(): jnp.einsum('hrl,tl->hrt', q_all, keys, precision=hp, preferred_element_ty...  11.2 us
    convert_element_type x2, other arithmetic, halves(): return (high.astype(jnp.bfloat16), (x - high).astype(jnp.bfloat16))  10.4 us
    dot_general x8, matrix products, dot(): left = jnp.dot(twice, both, preferred_element_type=jnp.float32)  9.35 us
    another operation x16, other arithmetic, gather(): held = jnp.stack([first, second], axis=1).reshape((-1,) + part.shape)  8.79 us
    dot_general x1, matrix products, on_device(): jnp.einsum('hrt,tl->hrl', expo, latent, precision=hp, preferred_element_t...  7.19 us
    unnamed x28, local copies, waits for them, and re-layouts  6.9 us
  transfers between devices with their start and end apart: 30, of which 21 were waited for; matrix products, arithmetic and copies ran while one was open for 22% of the time, Pallas kernels for 0%

profile of v2, /device:TPU:0, one launch (start us, length us, event | category | flops | bytes accessed | tf_op | source)
XLA Modules:
  0.0 172.0 jit_solution(2838888443928857688)
XLA Ops:
  1.8 3.0 %collective-permute-start = (f32[1,32,577]{2,1,0:T(8,128)S(1)}, f32[1,32,577]{2,1,0:T(8,128)S(1)}, u32[]{:S(2)}, u32[]{:S(2)}) collective-permute-start(f32[1,32,577]{2,1,0:T(8,128)S(1)} %fusion.52), channel_id=1, source_target_pairs={{0,8},{1,9},{2,10},{3,11},{4,12},{5,13},{6,14},{7,15},{8,0},{9,1},... | collective-permute-start | bytes 221576 | tf_op jit(solution)/shard_map/ppermute | solution.py:16
  4.8 2.4 %collective-permute-done = f32[1,32,577]{2,1,0:T(8,128)S(1)} collective-permute-done((f32[1,32,577]{2,1,0:T(8,128)S(1)}, f32[1,32,577]{2,1,0:T(8,128)S(1)}, u32[]{:S(2)}, u32[]{:S(2)}) %collective-permute-start) | collective-permute-done | bytes 73888 | tf_op jit(solution)/shard_map/ppermute | solution.py:16
  7.3 1.1 fusion.37
  8.3 2.1 %collective-permute-start.5 = (f32[1,32,577]{2,1,0:T(8,128)S(1)}, f32[1,32,577]{2,1,0:T(8,128)S(1)}, u32[]{:S(2)}, u32[]{:S(2)}) collective-permute-start(f32[1,32,577]{2,1,0:T(8,128)S(1)} %bitcast.277), channel_id=1, source_target_pairs={{0,8},{1,9},{2,10},{3,11},{4,12},{5,13},{6,14},{7,15},{8,0},{9,1},... | collective-permute-start | bytes 221576 | tf_op jit(solution)/shard_map/ppermute | solution.py:16
  10.4 2.7 %collective-permute-start.1 = (f32[2,32,577]{2,1,0:T(8,128)S(1)}, f32[2,32,577]{2,1,0:T(8,128)S(1)}, u32[]{:S(2)}, u32[]{:S(2)}) collective-permute-start(f32[2,32,577]{2,1,0:T(8,128)S(1)} %maximum_bitcast_fusion), channel_id=1, source_target_pairs={{0,16},{1,17},{2,18},{3,19},{4,20},{5,21},{6,22},{7,23},{8,24},{9,... | collective-permute-start | bytes 443144 | tf_op jit(solution)/shard_map/ppermute | solution.py:16
  13.6 3.0 %collective-permute-start.6 = (f32[2,32,577]{2,1,0:T(8,128)S(1)}, f32[2,32,577]{2,1,0:T(8,128)S(1)}, u32[]{:S(2)}, u32[]{:S(2)}) collective-permute-start(f32[2,32,577]{2,1,0:T(8,128)S(1)} %maximum_bitcast_fusion.1), channel_id=1, source_target_pairs={{0,16},{1,17},{2,18},{3,19},{4,20},{5,21},{6,22},{7,23},{8,24},{9,... | collective-permute-start | bytes 443144 | tf_op jit(solution)/shard_map/ppermute | solution.py:16
  16.6 7.3 %collective-permute-done.1 = f32[2,32,577]{2,1,0:T(8,128)S(1)} collective-permute-done((f32[2,32,577]{2,1,0:T(8,128)S(1)}, f32[2,32,577]{2,1,0:T(8,128)S(1)}, u32[]{:S(2)}, u32[]{:S(2)}) %collective-permute-start.1) | collective-permute-done | bytes 147744 | tf_op jit(solution)/shard_map/ppermute | solution.py:16
  23.9 2.5 %collective-permute-done.6 = f32[2,32,577]{2,1,0:T(8,128)S(1)} collective-permute-done((f32[2,32,577]{2,1,0:T(8,128)S(1)}, f32[2,32,577]{2,1,0:T(8,128)S(1)}, u32[]{:S(2)}, u32[]{:S(2)}) %collective-permute-start.6) | collective-permute-done | bytes 147744 | tf_op jit(solution)/shard_map/ppermute | solution.py:16
  26.5 1.6 collective-permute-start.2
  28.1 1.6 collective-permute-start.7
  29.7 5.7 %collective-permute-done.2 = f32[4,32,577]{2,1,0:T(8,128)S(1)} collective-permute-done((f32[4,32,577]{2,1,0:T(8,128)S(1)}, f32[4,32,577]{2,1,0:T(8,128)S(1)}, u32[]{:S(2)}, u32[]{:S(2)}) %collective-permute-start.2) | collective-permute-done | bytes 295456 | tf_op jit(solution)/shard_map/ppermute | solution.py:16
  36.3 1.5 collective-permute-start.3
  38.7 1.5 collective-permute-start.8
  40.3 10.3 %fusion.9 = (bf16[512,1792]{1,0:T(8,128)(2,1)}, bf16[512,1792]{1,0:T(8,128)(2,1)}, bf16[512,1792]{1,0:T(8,128)(2,1)}, bf16[512,1792]{1,0:T(8,128)(2,1)}, bf16[51...) fusion(f32[512,7168]{1,0:T(8,128)} %param.13), kind=kLoop, calls=%fused_computation.22 | loop fusion | flops 14680064 | bytes 29360128 | tf_op jit(solution)/shard_map/convert_element_type | solution.py:47
  50.6 2.3 %copy.58 = f32[256,768]{0,1:T(8,128)} copy(f32[256,768]{1,0:T(8,128)} %param.7) | data formatting | bytes 1572864 | tf_op args[0]
  52.9 1.4 select_bitcast_fusion.5
  54.4 1.2 copy.52
  55.5 1.2 bitcast_select_fusion.1
  56.9 1.2 copy.55
  60.5 1.0 copy.66
  61.5 2.1 %fusion.26 = f32[4,256,512]{2,1,0:T(8,128)S(1)} fusion(f32[4,512,128]{2,1,0:T(8,128)S(1)} %copy-done, f32[256,4,192]{0,2,1:T(8,128)} %bitcast.255), kind=kOutput, calls=%fused_computation.66 | convolution fusion | flops 402653184 | bytes 3670016 | tf_op jit(solution)/shard_map/rhn,hln->hrl/dot_general | solution.py:113
  63.6 1.9 %select_bitcast_fusion.3 = (f32[16,1,1,32,577]{4,3,0,2,1:T(8,128)S(1)}, f32[16,1,1,32,577]{4,3,0,2,1:T(8,128)S(1)}) fusion(f32[16,32,577]{2,1,0:T(8,128)} %collective-permute-done.4, pred[]{:T(512)S(6)} %eq.55, f32[8,2,1,32,577]{4,3,1,0,2:T(8,128)} %copy.52), kind=kLoop, calls=%fused_computation.51 | loop fusion | flops 590848 | bytes 4726785 | tf_op jit(solution)/shard_map/stack | solution.py:38
  65.9 1.9 %select_bitcast_fusion.1 = (f32[16,1,1,32,577]{4,3,0,2,1:T(8,128)S(1)}, f32[16,1,1,32,577]{4,3,0,2,1:T(8,128)S(1)}) fusion(f32[16,32,577]{2,1,0:T(8,128)} %collective-permute-done.9, pred[]{:T(512)S(6)} %eq.55, f32[4,2,2,32,577]{4,3,2,1,0:T(8,128)} %copy.55), kind=kLoop, calls=%fused_computation.49 | loop fusion | flops 590848 | bytes 4726785 | tf_op jit(solution)/shard_map/stack | solution.py:38
  70.5 11.2 %select_reduce_fusion = (f32[4,256]{1,0:T(4,128)S(1)}, f32[4,256,2048]{2,1,0:T(8,128)S(1)}) fusion(pred[256,2048]{1,0:T(8,128)(4,1)S(1)} %broadcast_compare_fusion, f32[2048,577]{1,0:T(8,128)S(1)} %bitcast.246, f32[4,256,64]{2,1,0:T(8,128)S(1)} %bitcast.274, f32[4,256,512]{2,1,0:T(8,128)S(1)} %fusion.26), kind=kOutput, calls=%fused_computation.1 | convolution fusion | flops 7252540416 | bytes 16003072 | tf_op jit(solution)/shard_map/hrl,tl->hrt/dot_general | solution.py:131
  81.7 2.0 %fusion = f32[4,256]{1,0:T(4,128)S(1)} fusion(f32[4,256,2048]{2,1,0:T(8,128)S(1)} %get-tuple-element.95, f32[4,256]{1,0:T(4,128)S(1)} %get-tuple-element.94, pred[256,2048]{1,0:T(8,128)(4,1)S(1)} %broadcast_compare_fusion), kind=kLoop, calls=%fused_computation.2 | loop fusion | flops 6290432 | bytes 8921088 | tf_op jit(solution)/shard_map/reduce_sum | solution.py:135
  83.7 7.2 %fusion.1 = f32[4,256,512]{2,1,0:T(8,128)S(1)} fusion(f32[4,256,2048]{2,1,0:T(8,128)S(1)} %get-tuple-element.95, f32[2048,577]{1,0:T(8,128)S(1)} %bitcast.247, f32[4,256]{1,0:T(4,128)S(1)} %get-tuple-element.94, pred[256,2048]{1,0:T(8,128)(4,1)S(1)} %broadcast_compare_fusion), kind=kOutput, calls=%fused_computation.3 | convolution fusion | flops 6446645248 | bytes 15208448 | tf_op jit(solution)/shard_map/hrt,tl->hrl/dot_general | solution.py:136
  90.9 1.1 fusion.19
  92.7 2.8 %fusion.15 = f32[128,1792]{1,0:T(8,128)S(1)} fusion(bf16[512,1792]{1,0:T(8,128)(2,1)} %get-tuple-element.58, bf16[512,1792]{1,0:T(8,128)(2,1)} %get-tuple-element.62, bf16[128,512]{1,0:T(8,128)(2,1)S(1)} %get-tuple-element.84), kind=kOutput, calls=%fused_computation.42 | convolution fusion | flops 477626368 | bytes 4718592 | tf_op jit(solution)/shard_map/dot_general | solution.py:70
  103.8 1.2 convolution_add_fusion.4
  107.6 1.0 copy-done.6
  111.0 4.0 %collective-permute-done.11 = f32[64,1792]{1,0:T(8,128)S(1)} collective-permute-done((f32[64,1792]{1,0:T(8,128)S(1)}, f32[64,1792]{1,0:T(8,128)S(1)}, u32[]{:S(2)}, u32[]{:S(2)}) %collective-permute-start.11) | collective-permute-done | bytes 458784 | tf_op jit(solution)/shard_map/ppermute | solution.py:16
  115.7 3.0 %collective-permute-done.16 = f32[64,1792]{1,0:T(8,128)S(1)} collective-permute-done((f32[64,1792]{1,0:T(8,128)S(1)}, f32[64,1792]{1,0:T(8,128)S(1)}, u32[]{:S(2)}, u32[]{:S(2)}) %collective-permute-start.16) | collective-permute-done | bytes 458784 | tf_op jit(solution)/shard_map/ppermute | solution.py:16
  118.8 1.2 collective-permute-start.17
  119.9 3.1 %collective-permute-done.12 = f32[32,1792]{1,0:T(8,128)S(1)} collective-permute-done((f32[32,1792]{1,0:T(8,128)S(1)}, f32[32,1792]{1,0:T(8,128)S(1)}, u32[]{:S(2)}, u32[]{:S(2)}) %collective-permute-start.12) | collective-permute-done | bytes 229408 | tf_op jit(solution)/shard_map/ppermute | solution.py:16
  123.2 1.8 %collective-permute-done.17 = f32[32,1792]{1,0:T(8,128)S(1)} collective-permute-done((f32[32,1792]{1,0:T(8,128)S(1)}, f32[32,1792]{1,0:T(8,128)S(1)}, u32[]{:S(2)}, u32[]{:S(2)}) %collective-permute-start.17) | collective-permute-done | bytes 229408 | tf_op jit(solution)/shard_map/ppermute | solution.py:16
  125.0 1.2 collective-permute-start.18
  126.2 6.5 %collective-permute-done.13 = f32[16,1792]{1,0:T(8,128)S(1)} collective-permute-done((f32[16,1792]{1,0:T(8,128)S(1)}, f32[16,1792]{1,0:T(8,128)S(1)}, u32[]{:S(2)}, u32[]{:S(2)}) %collective-permute-start.13) | collective-permute-done | bytes 114720 | tf_op jit(solution)/shard_map/ppermute | solution.py:16
  132.8 2.2 %collective-permute-done.18 = f32[16,1792]{1,0:T(8,128)S(1)} collective-permute-done((f32[16,1792]{1,0:T(8,128)S(1)}, f32[16,1792]{1,0:T(8,128)S(1)}, u32[]{:S(2)}, u32[]{:S(2)}) %collective-permute-start.18) | collective-permute-done | bytes 114720 | tf_op jit(solution)/shard_map/ppermute | solution.py:16
  135.2 1.8 %collective-permute-done.14 = f32[8,1792]{1,0:T(8,128)S(1)} collective-permute-done((f32[8,1792]{1,0:T(8,128)S(1)}, f32[8,1792]{1,0:T(8,128)S(1)}, u32[]{:S(2)}, u32[]{:S(2)}) %collective-permute-start.14) | collective-permute-done | bytes 57376 | tf_op jit(solution)/shard_map/ppermute | solution.py:16
  138.1 1.2 collective-permute-done.19
  140.1 8.3 %collective-permute-done.21 = f32[64,1792]{1,0:T(8,128)S(1)} collective-permute-done((f32[64,1792]{1,0:T(8,128)S(1)}, f32[64,1792]{1,0:T(8,128)S(1)}, u32[]{:S(2)}, u32[]{:S(2)}) %collective-permute-start.21) | collective-permute-done | bytes 458784 | tf_op jit(solution)/shard_map/ppermute | solution.py:16
  149.1 3.6 %collective-permute-done.26 = f32[64,1792]{1,0:T(8,128)S(1)} collective-permute-done((f32[64,1792]{1,0:T(8,128)S(1)}, f32[64,1792]{1,0:T(8,128)S(1)}, u32[]{:S(2)}, u32[]{:S(2)}) %collective-permute-start.26) | collective-permute-done | bytes 458784 | tf_op jit(solution)/shard_map/ppermute | solution.py:16
  153.7 2.1 %collective-permute-done.22 = f32[32,1792]{1,0:T(8,128)S(1)} collective-permute-done((f32[32,1792]{1,0:T(8,128)S(1)}, f32[32,1792]{1,0:T(8,128)S(1)}, u32[]{:S(2)}, u32[]{:S(2)}) %collective-permute-start.22) | collective-permute-done | bytes 229408 | tf_op jit(solution)/shard_map/ppermute | solution.py:16
  156.8 2.0 %collective-permute-done.27 = f32[32,1792]{1,0:T(8,128)S(1)} collective-permute-done((f32[32,1792]{1,0:T(8,128)S(1)}, f32[32,1792]{1,0:T(8,128)S(1)}, u32[]{:S(2)}, u32[]{:S(2)}) %collective-permute-start.27) | collective-permute-done | bytes 229408 | tf_op jit(solution)/shard_map/ppermute | solution.py:16
  159.0 6.7 %collective-permute-done.23 = f32[16,1792]{1,0:T(8,128)S(1)} collective-permute-done((f32[16,1792]{1,0:T(8,128)S(1)}, f32[16,1792]{1,0:T(8,128)S(1)}, u32[]{:S(2)}, u32[]{:S(2)}) %collective-permute-start.23) | collective-permute-done | bytes 114720 | tf_op jit(solution)/shard_map/ppermute | solution.py:16
  165.9 1.1 collective-permute-done.28
  168.0 2.0 %collective-permute-done.24 = f32[8,1792]{1,0:T(8,128)S(1)} collective-permute-done((f32[8,1792]{1,0:T(8,128)S(1)}, f32[8,1792]{1,0:T(8,128)S(1)}, u32[]{:S(2)}, u32[]{:S(2)}) %collective-permute-start.24) | collective-permute-done | bytes 57376 | tf_op jit(solution)/shard_map/ppermute | solution.py:16
  170.1 1.2 collective-permute-done.29
  (142 shorter events, 31.3 us)
Async XLA Ops:
  0.0 61.5 %copy-start = (f32[4,512,128]{2,1,0:T(8,128)S(1)}, f32[4,512,128]{2,1,0:T(8,128)}, u32[]{:S(2)}) copy-start(f32[4,512,128]{2,1,0:T(8,128)} %param.11) | copy-start | bytes 3145732
  1.8 5.5 %collective-permute-start = (f32[1,32,577]{2,1,0:T(8,128)S(1)}, f32[1,32,577]{2,1,0:T(8,128)S(1)}, u32[]{:S(2)}, u32[]{:S(2)}) collective-permute-start(f32[1,32,577]{2,1,0:T(8,128)S(1)} %fusion.52), channel_id=1, source_target_pairs={{0,8},{1,9},{2,10},{3,11},{4,12},{5,13},{6,14},{7,15},{8,0},{9,1},... | collective-permute-start | bytes 221576 | tf_op jit(solution)/shard_map/ppermute | solution.py:16
  8.3 5.2 %collective-permute-start.5 = (f32[1,32,577]{2,1,0:T(8,128)S(1)}, f32[1,32,577]{2,1,0:T(8,128)S(1)}, u32[]{:S(2)}, u32[]{:S(2)}) collective-permute-start(f32[1,32,577]{2,1,0:T(8,128)S(1)} %bitcast.277), channel_id=1, source_target_pairs={{0,8},{1,9},{2,10},{3,11},{4,12},{5,13},{6,14},{7,15},{8,0},{9,1},... | collective-permute-start | bytes 221576 | tf_op jit(solution)/shard_map/ppermute | solution.py:16
  10.4 13.5 %collective-permute-start.1 = (f32[2,32,577]{2,1,0:T(8,128)S(1)}, f32[2,32,577]{2,1,0:T(8,128)S(1)}, u32[]{:S(2)}, u32[]{:S(2)}) collective-permute-start(f32[2,32,577]{2,1,0:T(8,128)S(1)} %maximum_bitcast_fusion), channel_id=1, source_target_pairs={{0,16},{1,17},{2,18},{3,19},{4,20},{5,21},{6,22},{7,23},{8,24},{9,... | collective-permute-start | bytes 443144 | tf_op jit(solution)/shard_map/ppermute | solution.py:16
  13.6 12.8 %collective-permute-start.6 = (f32[2,32,577]{2,1,0:T(8,128)S(1)}, f32[2,32,577]{2,1,0:T(8,128)S(1)}, u32[]{:S(2)}, u32[]{:S(2)}) collective-permute-start(f32[2,32,577]{2,1,0:T(8,128)S(1)} %maximum_bitcast_fusion.1), channel_id=1, source_target_pairs={{0,16},{1,17},{2,18},{3,19},{4,20},{5,21},{6,22},{7,23},{8,24},{9,... | collective-permute-start | bytes 443144 | tf_op jit(solution)/shard_map/ppermute | solution.py:16
  26.5 8.8 %collective-permute-start.2 = (f32[4,32,577]{2,1,0:T(8,128)S(1)}, f32[4,32,577]{2,1,0:T(8,128)S(1)}, u32[]{:S(2)}, u32[]{:S(2)}) collective-permute-start(f32[4,32,577]{2,1,0:T(8,128)S(1)} %bitcast.264), channel_id=1, source_target_pairs={{0,4},{1,5},{2,6},{3,7},{4,0},{5,1},{6,2},{7,3},{8,12},{9,13},{10,... | collective-permute-start | bytes 886280 | tf_op jit(solution)/shard_map/ppermute | solution.py:16
  28.1 9.7 %collective-permute-start.7 = (f32[4,32,577]{2,1,0:T(8,128)S(1)}, f32[4,32,577]{2,1,0:T(8,128)S(1)}, u32[]{:S(2)}, u32[]{:S(2)}) collective-permute-start(f32[4,32,577]{2,1,0:T(8,128)S(1)} %bitcast.265), channel_id=1, source_target_pairs={{0,2},{1,3},{2,0},{3,1},{4,6},{5,7},{6,4},{7,5},{8,10},{9,11},{10,... | collective-permute-start | bytes 886280 | tf_op jit(solution)/shard_map/ppermute | solution.py:16
  36.3 16.6 %collective-permute-start.3 = (f32[8,32,577]{2,1,0:T(8,128)}, f32[8,32,577]{2,1,0:T(8,128)}, u32[]{:S(2)}, u32[]{:S(2)}) collective-permute-start(f32[8,32,577]{2,1,0:T(8,128)} %bitcast.13), channel_id=1, source_target_pairs={{0,2},{1,3},{2,0},{3,1},{4,6},{5,7},{6,4},{7,5},{8,10},{9,11},{10,... | collective-permute-start | bytes 1772552 | tf_op jit(solution)/shard_map/ppermute | solution.py:16
  38.7 16.8 %collective-permute-start.8 = (f32[8,32,577]{2,1,0:T(8,128)}, f32[8,32,577]{2,1,0:T(8,128)}, u32[]{:S(2)}, u32[]{:S(2)}) collective-permute-start(f32[8,32,577]{2,1,0:T(8,128)} %bitcast.32), channel_id=1, source_target_pairs={{0,4},{1,5},{2,6},{3,7},{4,0},{5,1},{6,2},{7,3},{8,12},{9,13},{10,... | collective-permute-start | bytes 1772552 | tf_op jit(solution)/shard_map/ppermute | solution.py:16
  55.5 8.1 %collective-permute-start.4 = (f32[16,32,577]{2,1,0:T(8,128)}, f32[16,32,577]{2,1,0:T(8,128)}, u32[]{:S(2)}, u32[]{:S(2)}) collective-permute-start(f32[16,32,577]{2,1,0:T(8,128)} %bitcast.16), channel_id=1, source_target_pairs={{0,1},{1,0},{2,3},{3,2},{4,5},{5,4},{6,7},{7,6},{8,9},{9,8},{10,11... | collective-permute-start | bytes 3545096 | tf_op jit(solution)/shard_map/ppermute | solution.py:16
  56.7 1.8 %copy-start.5 = (f32[256,768]{0,1:T(8,128)S(1)}, f32[256,768]{0,1:T(8,128)}, u32[]{:S(2)}) copy-start(f32[256,768]{0,1:T(8,128)} %copy.58) | copy-start | bytes 2359300
  58.0 7.9 %collective-permute-start.9 = (f32[16,32,577]{2,1,0:T(8,128)}, f32[16,32,577]{2,1,0:T(8,128)}, u32[]{:S(2)}, u32[]{:S(2)}) collective-permute-start(f32[16,32,577]{2,1,0:T(8,128)} %bitcast.34), channel_id=1, source_target_pairs={{0,1},{1,0},{2,3},{3,2},{4,5},{5,4},{6,7},{7,6},{8,9},{9,8},{10,11... | collective-permute-start | bytes 3545096 | tf_op jit(solution)/shard_map/ppermute | solution.py:16
  68.6 1.4 copy-start.11
  68.6 1.9 %copy-start.10 = (f32[256,4,64]{2,0,1:T(8,128)S(1)}, f32[256,4,64]{2,0,1:T(8,128)}, u32[]{:S(2)}) copy-start(f32[256,4,64]{2,0,1:T(8,128)} %copy.66) | copy-start | bytes 786436
  83.7 7.2 %copy-start.12 = (f32[4,512,128]{2,1,0:T(8,128)S(1)}, f32[4,512,128]{2,1,0:T(8,128)}, u32[]{:S(2)}) copy-start(f32[4,512,128]{2,1,0:T(8,128)} %param.12) | copy-start | bytes 3145732
  92.7 2.9 %copy-start.4 = (bf16[512,1792]{1,0:T(8,128)(2,1)S(1)}, bf16[512,1792]{1,0:T(8,128)(2,1)}, u32[]{:S(2)}) copy-start(bf16[512,1792]{1,0:T(8,128)(2,1)} %get-tuple-element.62) | copy-start | bytes 5505028
  92.7 3.1 %copy-start.9 = (bf16[512,1792]{1,0:T(8,128)(2,1)S(1)}, bf16[512,1792]{1,0:T(8,128)(2,1)}, u32[]{:S(2)}) copy-start(bf16[512,1792]{1,0:T(8,128)(2,1)} %get-tuple-element.58) | copy-start | bytes 5505028
  97.0 1.5 copy-start.3
  97.0 2.0 %copy-start.8 = (bf16[512,1792]{1,0:T(8,128)(2,1)S(1)}, bf16[512,1792]{1,0:T(8,128)(2,1)}, u32[]{:S(2)}) copy-start(bf16[512,1792]{1,0:T(8,128)(2,1)} %get-tuple-element.59) | copy-start | bytes 5505028
  97.0 4.9 %collective-permute-start.10 = (f32[128,1792]{1,0:T(8,128)S(1)}, f32[128,1792]{1,0:T(8,128)S(1)}, u32[]{:S(2)}, u32[]{:S(2)}) collective-permute-start(f32[128,1792]{1,0:T(8,128)S(1)} %convolution_add_fusion.5), channel_id=1, source_target_pairs={{0,1},{1,0},{2,3},{3,2},{4,5},{5,4},{6,7},{7,6},{8,9},{9,8},{10,11... | collective-permute-start | bytes 2752520 | tf_op jit(solution)/shard_map/ppermute | solution.py:16
  101.8 1.5 copy-start.2
  101.8 2.0 %copy-start.7 = (bf16[512,1792]{1,0:T(8,128)(2,1)S(1)}, bf16[512,1792]{1,0:T(8,128)(2,1)}, u32[]{:S(2)}) copy-start(bf16[512,1792]{1,0:T(8,128)(2,1)} %get-tuple-element.60) | copy-start | bytes 5505028
  101.8 3.6 %collective-permute-start.15 = (f32[128,1792]{1,0:T(8,128)S(1)}, f32[128,1792]{1,0:T(8,128)S(1)}, u32[]{:S(2)}, u32[]{:S(2)}) collective-permute-start(f32[128,1792]{1,0:T(8,128)S(1)} %convolution_add_fusion.3), channel_id=1, source_target_pairs={{0,1},{1,0},{2,3},{3,2},{4,5},{5,4},{6,7},{7,6},{8,9},{9,8},{10,11... | collective-permute-start | bytes 2752520 | tf_op jit(solution)/shard_map/ppermute | solution.py:16
  102.0 13.0 %collective-permute-start.11 = (f32[64,1792]{1,0:T(8,128)S(1)}, f32[64,1792]{1,0:T(8,128)S(1)}, u32[]{:S(2)}, u32[]{:S(2)}) collective-permute-start(f32[64,1792]{1,0:T(8,128)S(1)} %dynamic-slice_bitcast_fusion.1), channel_id=1, source_target_pairs={{0,2},{1,3},{2,0},{3,1},{4,6},{5,7},{6,4},{7,5},{8,10},{9,11},{10,... | collective-permute-start | bytes 1376264 | tf_op jit(solution)/shard_map/ppermute | solution.py:16
  105.6 13.1 %collective-permute-start.16 = (f32[64,1792]{1,0:T(8,128)S(1)}, f32[64,1792]{1,0:T(8,128)S(1)}, u32[]{:S(2)}, u32[]{:S(2)}) collective-permute-start(f32[64,1792]{1,0:T(8,128)S(1)} %bitcast.275), channel_id=1, source_target_pairs={{0,4},{1,5},{2,6},{3,7},{4,0},{5,1},{6,2},{7,3},{8,12},{9,13},{10,... | collective-permute-start | bytes 1376264 | tf_op jit(solution)/shard_map/ppermute | solution.py:16
  107.1 1.5 copy-start.6
  107.1 29.9 %collective-permute-start.20 = (f32[128,1792]{1,0:T(8,128)S(1)}, f32[128,1792]{1,0:T(8,128)S(1)}, u32[]{:S(2)}, u32[]{:S(2)}) collective-permute-start(f32[128,1792]{1,0:T(8,128)S(1)} %convolution_add_fusion.2), channel_id=1, source_target_pairs={{0,1},{1,0},{2,3},{3,2},{4,5},{5,4},{6,7},{7,6},{8,9},{9,8},{10,11... | collective-permute-start | bytes 2752520 | tf_op jit(solution)/shard_map/ppermute | solution.py:16
  109.6 29.8 %collective-permute-start.25 = (f32[128,1792]{1,0:T(8,128)S(1)}, f32[128,1792]{1,0:T(8,128)S(1)}, u32[]{:S(2)}, u32[]{:S(2)}) collective-permute-start(f32[128,1792]{1,0:T(8,128)S(1)} %convolution_add_fusion), channel_id=1, source_target_pairs={{0,1},{1,0},{2,3},{3,2},{4,5},{5,4},{6,7},{7,6},{8,9},{9,8},{10,11... | collective-permute-start | bytes 2752520 | tf_op jit(solution)/shard_map/ppermute | solution.py:16
  115.1 7.9 %collective-permute-start.12 = (f32[32,1792]{1,0:T(8,128)S(1)}, f32[32,1792]{1,0:T(8,128)S(1)}, u32[]{:S(2)}, u32[]{:S(2)}) collective-permute-start(f32[32,1792]{1,0:T(8,128)S(1)} %dynamic-slice_bitcast_fusion.5), channel_id=1, source_target_pairs={{0,4},{1,5},{2,6},{3,7},{4,0},{5,1},{6,2},{7,3},{8,12},{9,13},{10,... | collective-permute-start | bytes 688136 | tf_op jit(solution)/shard_map/ppermute | solution.py:16
  118.8 6.2 %collective-permute-start.17 = (f32[32,1792]{1,0:T(8,128)S(1)}, f32[32,1792]{1,0:T(8,128)S(1)}, u32[]{:S(2)}, u32[]{:S(2)}) collective-permute-start(f32[32,1792]{1,0:T(8,128)S(1)} %dynamic-slice_bitcast_fusion.4), channel_id=1, source_target_pairs={{0,2},{1,3},{2,0},{3,1},{4,6},{5,7},{6,4},{7,5},{8,10},{9,11},{10,... | collective-permute-start | bytes 688136 | tf_op jit(solution)/shard_map/ppermute | solution.py:16
  123.1 9.6 %collective-permute-start.13 = (f32[16,1792]{1,0:T(8,128)S(1)}, f32[16,1792]{1,0:T(8,128)S(1)}, u32[]{:S(2)}, u32[]{:S(2)}) collective-permute-start(f32[16,1792]{1,0:T(8,128)S(1)} %dynamic-slice_bitcast_fusion.9), channel_id=1, source_target_pairs={{0,16},{1,17},{2,18},{3,19},{4,20},{5,21},{6,22},{7,23},{8,24},{9,... | collective-permute-start | bytes 344072 | tf_op jit(solution)/shard_map/ppermute | solution.py:16
  125.0 10.1 %collective-permute-start.18 = (f32[16,1792]{1,0:T(8,128)S(1)}, f32[16,1792]{1,0:T(8,128)S(1)}, u32[]{:S(2)}, u32[]{:S(2)}) collective-permute-start(f32[16,1792]{1,0:T(8,128)S(1)} %dynamic-slice_bitcast_fusion.8), channel_id=1, source_target_pairs={{0,16},{1,17},{2,18},{3,19},{4,20},{5,21},{6,22},{7,23},{8,24},{9,... | collective-permute-start | bytes 344072 | tf_op jit(solution)/shard_map/ppermute | solution.py:16
  132.7 4.2 %collective-permute-start.14 = (f32[8,1792]{1,0:T(8,128)S(1)}, f32[8,1792]{1,0:T(8,128)S(1)}, u32[]{:S(2)}, u32[]{:S(2)}) collective-permute-start(f32[8,1792]{1,0:T(8,128)S(1)} %dynamic-slice_bitcast_fusion.13), channel_id=1, source_target_pairs={{0,8},{1,9},{2,10},{3,11},{4,12},{5,13},{6,14},{7,15},{8,0},{9,1},... | collective-permute-start | bytes 172040 | tf_op jit(solution)/shard_map/ppermute | solution.py:16
  135.1 4.2 %collective-permute-start.19 = (f32[8,1792]{1,0:T(8,128)S(1)}, f32[8,1792]{1,0:T(8,128)S(1)}, u32[]{:S(2)}, u32[]{:S(2)}) collective-permute-start(f32[8,1792]{1,0:T(8,128)S(1)} %dynamic-slice_bitcast_fusion.12), channel_id=1, source_target_pairs={{0,8},{1,9},{2,10},{3,11},{4,12},{5,13},{6,14},{7,15},{8,0},{9,1},... | collective-permute-start | bytes 172040 | tf_op jit(solution)/shard_map/ppermute | solution.py:16
  137.2 11.3 %collective-permute-start.21 = (f32[64,1792]{1,0:T(8,128)S(1)}, f32[64,1792]{1,0:T(8,128)S(1)}, u32[]{:S(2)}, u32[]{:S(2)}) collective-permute-start(f32[64,1792]{1,0:T(8,128)S(1)} %dynamic-slice_bitcast_fusion), channel_id=1, source_target_pairs={{0,2},{1,3},{2,0},{3,1},{4,6},{5,7},{6,4},{7,5},{8,10},{9,11},{10,... | collective-permute-start | bytes 1376264 | tf_op jit(solution)/shard_map/ppermute | solution.py:16
  139.5 13.1 %collective-permute-start.26 = (f32[64,1792]{1,0:T(8,128)S(1)}, f32[64,1792]{1,0:T(8,128)S(1)}, u32[]{:S(2)}, u32[]{:S(2)}) collective-permute-start(f32[64,1792]{1,0:T(8,128)S(1)} %bitcast.276), channel_id=1, source_target_pairs={{0,4},{1,5},{2,6},{3,7},{4,0},{5,1},{6,2},{7,3},{8,12},{9,13},{10,... | collective-permute-start | bytes 1376264 | tf_op jit(solution)/shard_map/ppermute | solution.py:16
  148.5 7.3 %collective-permute-start.22 = (f32[32,1792]{1,0:T(8,128)S(1)}, f32[32,1792]{1,0:T(8,128)S(1)}, u32[]{:S(2)}, u32[]{:S(2)}) collective-permute-start(f32[32,1792]{1,0:T(8,128)S(1)} %dynamic-slice_bitcast_fusion.3), channel_id=1, source_target_pairs={{0,4},{1,5},{2,6},{3,7},{4,0},{5,1},{6,2},{7,3},{8,12},{9,13},{10,... | collective-permute-start | bytes 688136 | tf_op jit(solution)/shard_map/ppermute | solution.py:16
  152.7 19.3 %copy-start.1 = (f32[4,512,128]{2,1,0:T(8,128)S(1)}, f32[4,512,128]{2,1,0:T(8,128)}, u32[]{:S(2)}) copy-start(f32[4,512,128]{2,1,0:T(8,128)} %param.11) | copy-start | bytes 3145732
  152.8 6.1 %collective-permute-start.27 = (f32[32,1792]{1,0:T(8,128)S(1)}, f32[32,1792]{1,0:T(8,128)S(1)}, u32[]{:S(2)}, u32[]{:S(2)}) collective-permute-start(f32[32,1792]{1,0:T(8,128)S(1)} %dynamic-slice_bitcast_fusion.2), channel_id=1, source_target_pairs={{0,2},{1,3},{2,0},{3,1},{4,6},{5,7},{6,4},{7,5},{8,10},{9,11},{10,... | collective-permute-start | bytes 688136 | tf_op jit(solution)/shard_map/ppermute | solution.py:16
  155.9 9.9 %collective-permute-start.23 = (f32[16,1792]{1,0:T(8,128)S(1)}, f32[16,1792]{1,0:T(8,128)S(1)}, u32[]{:S(2)}, u32[]{:S(2)}) collective-permute-start(f32[16,1792]{1,0:T(8,128)S(1)} %dynamic-slice_bitcast_fusion.7), channel_id=1, source_target_pairs={{0,16},{1,17},{2,18},{3,19},{4,20},{5,21},{6,22},{7,23},{8,24},{9,... | collective-permute-start | bytes 344072 | tf_op jit(solution)/shard_map/ppermute | solution.py:16
  158.9 8.1 %collective-permute-start.28 = (f32[16,1792]{1,0:T(8,128)S(1)}, f32[16,1792]{1,0:T(8,128)S(1)}, u32[]{:S(2)}, u32[]{:S(2)}) collective-permute-start(f32[16,1792]{1,0:T(8,128)S(1)} %dynamic-slice_bitcast_fusion.6), channel_id=1, source_target_pairs={{0,16},{1,17},{2,18},{3,19},{4,20},{5,21},{6,22},{7,23},{8,24},{9,... | collective-permute-start | bytes 344072 | tf_op jit(solution)/shard_map/ppermute | solution.py:16
  165.8 4.2 %collective-permute-start.24 = (f32[8,1792]{1,0:T(8,128)S(1)}, f32[8,1792]{1,0:T(8,128)S(1)}, u32[]{:S(2)}, u32[]{:S(2)}) collective-permute-start(f32[8,1792]{1,0:T(8,128)S(1)} %dynamic-slice_bitcast_fusion.11), channel_id=1, source_target_pairs={{0,8},{1,9},{2,10},{3,11},{4,12},{5,13},{6,14},{7,15},{8,0},{9,1},... | collective-permute-start | bytes 172040 | tf_op jit(solution)/shard_map/ppermute | solution.py:16
  167.0 4.2 %collective-permute-start.29 = (f32[8,1792]{1,0:T(8,128)S(1)}, f32[8,1792]{1,0:T(8,128)S(1)}, u32[]{:S(2)}, u32[]{:S(2)}) collective-permute-start(f32[8,1792]{1,0:T(8,128)S(1)} %dynamic-slice_bitcast_fusion.10), channel_id=1, source_target_pairs={{0,8},{1,9},{2,10},{3,11},{4,12},{5,13},{6,14},{7,15},{8,0},{9,1},... | collective-permute-start | bytes 172040 | tf_op jit(solution)/shard_map/ppermute | solution.py:16
